TPU v7x, 32 devices: a whole 2x2x4 slice. The times are simulated.
32 devices in a mesh: dp: 16 (over z, x, core), seq: 2 (over y).
Axes of the slice: x: 2, y: 2, z: 4, core: 2. Of those that a mesh axis runs over, the one named last changes fastest.
Arguments:
- inputs: bfloat16 [16, 1024, 1024], P('dp', 'seq'), may hold values from -6 to 6
- doc_ids: int32 [16, 1024], P('dp', 'seq'), may hold values from 0 to 7, never falling along the last dimension, each value on 1 to 256 neighbouring positions
- w_qkv: bfloat16 [1024, 3072], replicated, may hold values from -0.1875 to 0.1875
- bias_q: bfloat16 [1024], replicated, may hold values from -3 to 3
- bias_v: bfloat16 [1024], replicated, may hold values from -3 to 3
- w_out: bfloat16 [1024, 1024], replicated, may hold values from -0.375 to 0.375
- bias_out: bfloat16 [1024], replicated, may hold values from -2 to 2
- norm1_gain: bfloat16 [1024], replicated, may hold values from 0.5 to 1.5
- norm1_bias: bfloat16 [1024], replicated, may hold values from -2 to 2
- norm2_gain: bfloat16 [1024], replicated, may hold values from 0.5 to 1.5
- norm2_bias: bfloat16 [1024], replicated, may hold values from -2 to 2
- w_up: bfloat16 [1024, 4096], replicated, may hold values from -0.1875 to 0.1875
- bias_up: bfloat16 [4096], replicated, may hold values from -2 to 2
- w_down: bfloat16 [4096, 1024], replicated, may hold values from -0.125 to 0.125
- bias_down: bfloat16 [1024], replicated, may hold values from -2 to 2
- cotangent: bfloat16 [16, 1024, 1024], P('dp', 'seq'), may hold values from -6 to 6
Outputs:
- out: bfloat16 [16, 1024, 1024], P('dp', 'seq')
- grad_inputs: float32 [16, 1024, 1024], P('dp', 'seq')
- grad_w_qkv: float32 [1024, 3072], P('dp', 'seq')
- grad_bias_q: float32 [1024], replicated
- grad_bias_v: float32 [1024], replicated
- grad_w_out: float32 [1024, 1024], P('dp', 'seq')
- grad_bias_out: float32 [1024], replicated
- grad_norm1_gain: float32 [1024], replicated
- grad_norm1_bias: float32 [1024], replicated
- grad_norm2_gain: float32 [1024], replicated
- grad_norm2_bias: float32 [1024], replicated
- grad_w_up: float32 [1024, 4096], P('dp', 'seq')
- grad_bias_up: float32 [4096], replicated
- grad_w_down: float32 [4096, 1024], P('dp', 'seq')
- grad_bias_down: float32 [1024], replicated
Inputs may be any that keep to these rules, and one draw needn't show every extreme that they name: `doc_ids`: non-decreasing along each row; each row holds 8 documents of 1 to 256 tokens, one of exactly 256.
All inputs are finite; a program needn't handle non-finite values.
Results may differ from a plain program's by a relative error of at most 0.017.
Values may be sent and summed in bfloat16 or wider, within the bound.
A program may use at most 192 MiB of HBM per device.

v0:
```python
import jax
import jax.numpy as jnp
from jax import lax
from jax.sharding import PartitionSpec as P

HEAD_DIM = 128


norm_eps = 1e-05
masked_score = -1e30


def smooth_act(values):
    return jax.nn.gelu(values, approximate=True)


def layer_norm(values, norm_gain, norm_shift):
    center = values - jnp.mean(values, axis=-1, keepdims=True)
    inv_std = lax.rsqrt(jnp.mean(center * center, axis=-1, keepdims=True) + norm_eps)
    normed = center * inv_std
    return (normed * norm_gain + norm_shift, normed, inv_std)


def norm_back(grad_out, normed, inv_std, norm_gain):
    grad_gain = jnp.sum(grad_out * normed, axis=0)
    grad_shift = jnp.sum(grad_out, axis=0)
    inner_grad = grad_out * norm_gain
    grad_in = inv_std * (
        inner_grad
        - jnp.mean(inner_grad, axis=-1, keepdims=True)
        - normed * jnp.mean(inner_grad * normed, axis=-1, keepdims=True)
    )
    return (grad_in, grad_gain, grad_shift)


def block_scores(query_block, key_rows, first_row, head_slope, row_docs):
    block_rows = query_block.shape[0]
    length = key_rows.shape[0]
    raw_scores = lax.dot_general(
        query_block, key_rows, (((1,), (1,)), ((), ())), preferred_element_type=jnp.float32
    )
    query_pos = first_row + jnp.arange(block_rows, dtype=jnp.int32)
    key_pos = jnp.arange(length, dtype=jnp.int32)
    offset = query_pos[:, None] - key_pos[None, :]
    query_doc = lax.dynamic_slice_in_dim(row_docs, first_row, block_rows)
    allowed = (offset >= 0) & (query_doc[:, None] == row_docs[None, :])
    scores = raw_scores * key_rows.shape[1] ** (-0.5) - head_slope * offset.astype(jnp.float32)
    return jnp.where(allowed, scores, masked_score)


def head_forward(query_rows, key_rows, value_rows, head_slope, row_docs, block_rows):
    starts = jnp.arange(query_rows.shape[0] // block_rows, dtype=jnp.int32) * block_rows

    def one_block(first_row):
        query_block = lax.dynamic_slice_in_dim(query_rows, first_row, block_rows)
        scores = block_scores(query_block, key_rows, first_row, head_slope, row_docs)
        row_max = jnp.max(scores, axis=-1, keepdims=True)
        exponent = jnp.exp(scores - row_max)
        row_total = jnp.sum(exponent, axis=-1, keepdims=True)
        weights = (exponent / row_total).astype(jnp.bfloat16)
        block_out = jnp.dot(weights, value_rows, preferred_element_type=jnp.float32).astype(
            jnp.bfloat16
        )
        return (block_out, (row_max + jnp.log(row_total))[:, 0])

    block_outs, log_total = lax.map(one_block, starts)
    return (block_outs.reshape(-1, value_rows.shape[1]), log_total.reshape(-1))


def head_backward(
    query_rows, key_rows, value_rows, grad_rows, log_total, head_slope, row_docs, block_rows
):
    length, head_width = key_rows.shape
    inv_root = head_width ** (-0.5)
    starts = jnp.arange(length // block_rows, dtype=jnp.int32) * block_rows

    def one_block(running, first_row):
        grad_keys, grad_values = running
        query_block = lax.dynamic_slice_in_dim(query_rows, first_row, block_rows)
        grad_block = lax.dynamic_slice_in_dim(grad_rows, first_row, block_rows)
        total_block = lax.dynamic_slice_in_dim(log_total, first_row, block_rows)
        scores = block_scores(query_block, key_rows, first_row, head_slope, row_docs)
        weights = jnp.exp(scores - total_block[:, None])
        grad_weights = lax.dot_general(
            grad_block, value_rows, (((1,), (1,)), ((), ())), preferred_element_type=jnp.float32
        )
        inner_sum = jnp.sum(weights * grad_weights, axis=-1, keepdims=True)
        grad_scores = (weights * (grad_weights - inner_sum)).astype(jnp.bfloat16)
        grad_query = jnp.dot(grad_scores, key_rows, preferred_element_type=jnp.float32) * inv_root
        grad_keys = (
            grad_keys
            + lax.dot_general(
                grad_scores,
                query_block,
                (((0,), (0,)), ((), ())),
                preferred_element_type=jnp.float32,
            )
            * inv_root
        )
        grad_values = grad_values + lax.dot_general(
            weights.astype(jnp.bfloat16),
            grad_block,
            (((0,), (0,)), ((), ())),
            preferred_element_type=jnp.float32,
        )
        return ((grad_keys, grad_values), grad_query)

    zeros_block = jnp.zeros((length, head_width), jnp.float32)
    (grad_keys, grad_values), grad_query = lax.scan(one_block, (zeros_block, zeros_block), starts)
    return (
        grad_query.reshape(length, head_width).astype(jnp.bfloat16),
        grad_keys.astype(jnp.bfloat16),
        grad_values.astype(jnp.bfloat16),
    )


def local(
    inputs,
    doc_ids,
    w_qkv,
    bias_q,
    bias_v,
    w_out,
    bias_out,
    norm1_gain,
    norm1_bias,
    norm2_gain,
    norm2_bias,
    w_up,
    bias_up,
    w_down,
    bias_down,
    cotangent,
):
    model_width = w_out.shape[0]
    tokens = inputs.shape[1]
    head_count = model_width // HEAD_DIM
    float_inputs = inputs[0].astype(jnp.float32)
    gain_one = norm1_gain.astype(jnp.float32)
    gain_two = norm2_gain.astype(jnp.float32)
    normed_in, normed_one, inv_one = layer_norm(
        float_inputs, gain_one, norm1_bias.astype(jnp.float32)
    )
    act_one = normed_in.astype(jnp.bfloat16)
    projected = jnp.dot(act_one, w_qkv, preferred_element_type=jnp.float32)
    query_rows = (projected[:, :model_width] + bias_q.astype(jnp.float32)).astype(jnp.bfloat16)
    key_rows = projected[:, model_width : 2 * model_width].astype(jnp.bfloat16)
    value_rows = (projected[:, 2 * model_width :] + bias_v.astype(jnp.float32)).astype(jnp.bfloat16)
    query_rows = query_rows.reshape(tokens, head_count, HEAD_DIM)
    key_rows = key_rows.reshape(tokens, head_count, HEAD_DIM)
    value_rows = value_rows.reshape(tokens, head_count, HEAD_DIM)
    whole_q, whole_k, whole_v = (
        lax.all_to_all(query_rows, "seq", split_axis=1, concat_axis=0, tiled=True),
        lax.all_to_all(key_rows, "seq", split_axis=1, concat_axis=0, tiled=True),
        lax.all_to_all(value_rows, "seq", split_axis=1, concat_axis=0, tiled=True),
    )
    row_docs = lax.all_gather(doc_ids, "seq", axis=1, tiled=True)[0]
    local_heads = whole_q.shape[1]
    length = whole_q.shape[0]
    block_rows = min(512, length)
    first_head = lax.axis_index("seq") * local_heads
    slopes = jnp.exp2(
        -(first_head + 1 + jnp.arange(local_heads, dtype=jnp.int32)).astype(jnp.float32)
    )
    head_q = jnp.moveaxis(whole_q, 1, 0)
    head_k = jnp.moveaxis(whole_k, 1, 0)
    head_v = jnp.moveaxis(whole_v, 1, 0)

    def forward_head(operands):
        return head_forward(
            operands[0], operands[1], operands[2], operands[3], row_docs, block_rows
        )

    head_outs, head_totals = lax.map(forward_head, (head_q, head_k, head_v, slopes))
    mixed_heads = lax.all_to_all(
        jnp.moveaxis(head_outs, 0, 1), "seq", split_axis=0, concat_axis=1, tiled=True
    )
    mixed_flat = mixed_heads.reshape(tokens, model_width)
    second = (
        float_inputs
        + jnp.dot(mixed_flat, w_out, preferred_element_type=jnp.float32)
        + bias_out.astype(jnp.float32)
    )
    normed_mid, normed_two, inv_two = layer_norm(second, gain_two, norm2_bias.astype(jnp.float32))
    act_two = normed_mid.astype(jnp.bfloat16)
    pre_act = jnp.dot(act_two, w_up, preferred_element_type=jnp.float32) + bias_up.astype(
        jnp.float32
    )
    activated, act_pullback = jax.vjp(smooth_act, pre_act)
    hidden = activated.astype(jnp.bfloat16)
    result = (
        second
        + jnp.dot(hidden, w_down, preferred_element_type=jnp.float32)
        + bias_down.astype(jnp.float32)
    )
    grad_out = cotangent[0].astype(jnp.float32)
    grad_low = grad_out.astype(jnp.bfloat16)
    g_bias_down = jnp.sum(grad_low.astype(jnp.float32), axis=0)
    g_w_down = lax.dot_general(
        hidden, grad_low, (((0,), (0,)), ((), ())), preferred_element_type=jnp.float32
    )
    grad_hidden = lax.dot_general(
        grad_low, w_down, (((1,), (1,)), ((), ())), preferred_element_type=jnp.float32
    )
    grad_pre = act_pullback(grad_hidden)[0].astype(jnp.bfloat16)
    g_bias_up = jnp.sum(grad_pre.astype(jnp.float32), axis=0)
    g_w_up = lax.dot_general(
        act_two, grad_pre, (((0,), (0,)), ((), ())), preferred_element_type=jnp.float32
    )
    grad_norm_two = lax.dot_general(
        grad_pre, w_up, (((1,), (1,)), ((), ())), preferred_element_type=jnp.float32
    )
    grad_mid, g_gain_two, g_shift_two = norm_back(grad_norm_two, normed_two, inv_two, gain_two)
    grad_second = grad_out + grad_mid
    grad_branch = grad_second.astype(jnp.bfloat16)
    g_bias_out = jnp.sum(grad_branch.astype(jnp.float32), axis=0)
    g_w_out = lax.dot_general(
        mixed_flat, grad_branch, (((0,), (0,)), ((), ())), preferred_element_type=jnp.float32
    )
    grad_mixed = lax.dot_general(
        grad_branch, w_out, (((1,), (1,)), ((), ())), preferred_element_type=jnp.float32
    ).astype(jnp.bfloat16)
    grad_whole = lax.all_to_all(
        grad_mixed.reshape(tokens, head_count, HEAD_DIM),
        "seq",
        split_axis=1,
        concat_axis=0,
        tiled=True,
    )
    grad_heads = jnp.moveaxis(grad_whole, 1, 0)

    def backward_head(operands):
        return head_backward(
            operands[0],
            operands[1],
            operands[2],
            operands[3],
            operands[4],
            operands[5],
            row_docs,
            block_rows,
        )

    grad_q, grad_k, grad_v = lax.map(
        backward_head, (head_q, head_k, head_v, grad_heads, head_totals, slopes)
    )
    back_q, back_k, back_v = (
        lax.all_to_all(jnp.moveaxis(grad_q, 0, 1), "seq", split_axis=0, concat_axis=1, tiled=True),
        lax.all_to_all(jnp.moveaxis(grad_k, 0, 1), "seq", split_axis=0, concat_axis=1, tiled=True),
        lax.all_to_all(jnp.moveaxis(grad_v, 0, 1), "seq", split_axis=0, concat_axis=1, tiled=True),
    )
    back_q = back_q.reshape(tokens, model_width)
    back_k = back_k.reshape(tokens, model_width)
    back_v = back_v.reshape(tokens, model_width)
    g_bias_q = jnp.sum(back_q.astype(jnp.float32), axis=0)
    g_bias_v = jnp.sum(back_v.astype(jnp.float32), axis=0)
    grad_proj = jnp.concatenate([back_q, back_k, back_v], axis=1)
    g_w_qkv = lax.dot_general(
        act_one, grad_proj, (((0,), (0,)), ((), ())), preferred_element_type=jnp.float32
    )
    grad_norm_one = lax.dot_general(
        grad_proj, w_qkv, (((1,), (1,)), ((), ())), preferred_element_type=jnp.float32
    )
    grad_first, g_gain_one, g_shift_one = norm_back(grad_norm_one, normed_one, inv_one, gain_one)
    grad_inputs = grad_second + grad_first
    matrices = (g_w_qkv, g_w_out, g_w_up, g_w_down)
    partial_sums = (
        lax.psum_scatter(
            matrices[0].astype(jnp.bfloat16), "dp", scatter_dimension=0, tiled=True
        ).astype(jnp.float32),
        lax.psum_scatter(
            matrices[1].astype(jnp.bfloat16), "dp", scatter_dimension=0, tiled=True
        ).astype(jnp.float32),
        lax.psum_scatter(
            matrices[2].astype(jnp.bfloat16), "dp", scatter_dimension=0, tiled=True
        ).astype(jnp.float32),
        lax.psum_scatter(
            matrices[3].astype(jnp.bfloat16), "dp", scatter_dimension=0, tiled=True
        ).astype(jnp.float32),
    )
    summed = (
        lax.psum_scatter(
            partial_sums[0].astype(jnp.bfloat16), "seq", scatter_dimension=1, tiled=True
        ).astype(jnp.float32),
        lax.psum_scatter(
            partial_sums[1].astype(jnp.bfloat16), "seq", scatter_dimension=1, tiled=True
        ).astype(jnp.float32),
        lax.psum_scatter(
            partial_sums[2].astype(jnp.bfloat16), "seq", scatter_dimension=1, tiled=True
        ).astype(jnp.float32),
        lax.psum_scatter(
            partial_sums[3].astype(jnp.bfloat16), "seq", scatter_dimension=1, tiled=True
        ).astype(jnp.float32),
    )
    vectors = lax.psum(
        (
            g_bias_q,
            g_bias_v,
            g_bias_out,
            g_gain_one,
            g_shift_one,
            g_gain_two,
            g_shift_two,
            g_bias_up,
            g_bias_down,
        ),
        ("dp", "seq"),
    )
    return (
        result.astype(jnp.bfloat16)[None],
        grad_inputs[None],
        summed[0],
        vectors[0],
        vectors[1],
        summed[1],
        vectors[2],
        vectors[3],
        vectors[4],
        vectors[5],
        vectors[6],
        summed[2],
        vectors[7],
        summed[3],
        vectors[8],
    )


def solution(mesh):
    in_specs = (
        P("dp", "seq", None),
        P("dp", "seq"),
        P(),
        P(),
        P(),
        P(),
        P(),
        P(),
        P(),
        P(),
        P(),
        P(),
        P(),
        P(),
        P(),
        P("dp", "seq", None),
    )
    out_specs = (
        P("dp", "seq", None),
        P("dp", "seq", None),
        P("dp", "seq"),
        P(),
        P(),
        P("dp", "seq"),
        P(),
        P(),
        P(),
        P(),
        P(),
        P("dp", "seq"),
        P(),
        P("dp", "seq"),
        P(),
    )
    return jax.shard_map(local, mesh=mesh, in_specs=in_specs, out_specs=out_specs, check_vma=False)
```

profile of v0, /device:TPU:0, one launch (start us, length us, event | category | flops | bytes accessed | tf_op | source)
XLA Modules:
  0.0 835.3 jit_solution(12405552678172688110)
XLA Ops:
  10.6 5.8 fusion.65
  27.4 12.7 %all-to-all-done = bf16[512,8,128]{2,0,1:T(8,128)(2,1)} async-done(((bf16[512,8,128]{2,0,1:T(8,128)(2,1)}), bf16[512,8,128]{2,0,1:T(8,128)(2,1)}, u32[]{:S(2)}, u32[]{:S(2)}) %all-to-all-start) | async-done | bytes 1048608 | tf_op jit(solution)/shard_map/all_to_all | solution.py:153
  47.3 10.7 %all-to-all-done.2 = bf16[512,8,128]{2,0,1:T(8,128)(2,1)} async-done(((bf16[512,8,128]{2,0,1:T(8,128)(2,1)}), bf16[512,8,128]{2,0,1:T(8,128)(2,1)}, u32[]{:S(2)}, u32[]{:S(2)}) %all-to-all-start.2) | async-done | bytes 1048608 | tf_op jit(solution)/shard_map/all_to_all | solution.py:155
  62.5 12.5 %all_gather.3 = s32[1,1024]{1,0:T(1,128)S(1)} all-gather(s32[1,512]{1,0:T(1,128)S(1)} %copy-done.54), channel_id=1, replica_groups=mesh['dp'=16,'seq'=2] {'seq'}, dimensions={1}, use_global_device_ids=true | all-gather | bytes 6144 | tf_op jit(solution)/shard_map/all_gather | solution.py:157
  83.0 116.2 %while.54 = (s32[]{:T(128)}, bf16[4,1024,128]{2,1,0:T(8,128)(2,1)}, f32[4,1024]{1,0:T(4,128)S(1)}, bf16[4,1024,128]{2,1,0:T(8,128)(2,1)}, bf16[4,1024,128]{2,1,0...) while((s32[]{:T(128)}, bf16[4,1024,128]{2,1,0:T(8,128)(2,1)}, ...), condition=%wide.region_7.8_spmd, body=%wide.region_2.7_spmd.sunk | while | flops 276365312 | bytes 9227732 | solution.py:174
  86.4 23.9 %while.57 = (s32[]{:T(128)}, bf16[2,512,128]{2,1,0:T(8,128)(2,1)}, f32[2,512]{1,0:T(2,128)S(1)}, s32[2]{0:T(128)S(1)}, s32[1024]{0:T(1024)S(1)}, /*index=5*/s32[...) while((s32[]{:T(128)}, bf16[2,512,128]{2,1,0:T(8,128)(2,1)}, ...), condition=%wide.region_6.6_spmd, body=%wide.region_3.5_spmd.sunk | while | flops 276365312 | bytes 7113407 | solution.py:66
  115.5 23.9 %while.57 = (s32[]{:T(128)}, bf16[2,512,128]{2,1,0:T(8,128)(2,1)}, f32[2,512]{1,0:T(2,128)S(1)}, s32[2]{0:T(128)S(1)}, s32[1024]{0:T(1024)S(1)}, /*index=5*/s32[...) while((s32[]{:T(128)}, bf16[2,512,128]{2,1,0:T(8,128)(2,1)}, ...), condition=%wide.region_6.6_spmd, body=%wide.region_3.5_spmd.sunk | while | flops 276365312 | bytes 7113407 | solution.py:66
  144.6 23.9 %while.57 = (s32[]{:T(128)}, bf16[2,512,128]{2,1,0:T(8,128)(2,1)}, f32[2,512]{1,0:T(2,128)S(1)}, s32[2]{0:T(128)S(1)}, s32[1024]{0:T(1024)S(1)}, /*index=5*/s32[...) while((s32[]{:T(128)}, bf16[2,512,128]{2,1,0:T(8,128)(2,1)}, ...), condition=%wide.region_6.6_spmd, body=%wide.region_3.5_spmd.sunk | while | flops 276365312 | bytes 7113407 | solution.py:66
  173.6 23.9 %while.57 = (s32[]{:T(128)}, bf16[2,512,128]{2,1,0:T(8,128)(2,1)}, f32[2,512]{1,0:T(2,128)S(1)}, s32[2]{0:T(128)S(1)}, s32[1024]{0:T(1024)S(1)}, /*index=5*/s32[...) while((s32[]{:T(128)}, bf16[2,512,128]{2,1,0:T(8,128)(2,1)}, ...), condition=%wide.region_6.6_spmd, body=%wide.region_3.5_spmd.sunk | while | flops 276365312 | bytes 7113407 | solution.py:66
  202.3 5.0 all-to-all-start.3
  207.4 11.6 %all-to-all-done.3 = bf16[1024,4,128]{2,1,0:T(4,128)(2,1)} async-done(((bf16[1024,4,128]{2,1,0:T(4,128)(2,1)}), bf16[1024,4,128]{2,1,0:T(4,128)(2,1)}, u32[]{:S(2)}, u32[]{:S(2)}) %all-to-all-start.3) | async-done | bytes 1048608 | tf_op jit(solution)/shard_map/all_to_all | solution.py:175
  226.6 10.7 %fusion.67 = f32[512,4096]{1,0:T(8,128)} fusion(bf16[1024,4096]{1,0:T(8,128)(2,1)} %param.35, f32[512,1024]{1,0:T(8,128)S(1)} %get-tuple-element.415, f32[1024]{0:T(1024)S(1)} %convert_element_type.164, f32[1024]{0:T(1024)S(1)} %convert_element_type.163, f32[512]{0:T(512)S(1)} %add_rsqrt_fusion, f32[512]{0:T(512)S(1)} %broadcast_multiply_fusion.4), kind=kOutput, calls=%fused_computation.137 | convolution fusion | flops 4297588736 | bytes 18886656 | tf_op jit(solution)/shard_map/dot_general | solution.py:186
  237.4 16.2 %convert_reduce_fusion = (f32[4096]{0:T(1024)}, bf16[512,4096]{1,0:T(8,128)(2,1)}) fusion(f32[512,4096]{1,0:T(8,128)} %fusion.67, f32[4096]{0:T(1024)S(1)} %convert_element_type.166, bf16[4096,1024]{1,0:T(8,128)(2,1)} %param.37, bf16[1,512,1024]{2,1,0:T(8,128)(2,1)S(1)} %copy-done.25), kind=kOutput, calls=%fused_computation.60 | convolution fusion | flops 4343197696 | bytes 22052864 | tf_op jit(solution)/shard_map/dot_general | solution.py:202
  253.6 7.8 multiply_reduce_fusion.1
  273.1 6.9 all-to-all-done.4
  283.4 128.2 %while.56 = (s32[]{:T(128)}, bf16[4,1024,128]{2,1,0:T(8,128)(2,1)}, bf16[4,1024,128]{2,1,0:T(8,128)(2,1)}, bf16[4,1024,128]{2,1,0:T(8,128)(2,1)}, bf16[4,1024,12...) while((s32[]{:T(128)}, bf16[4,1024,128]{2,1,0:T(8,128)(2,1)}, ...), condition=%wide.region_16.17_spmd, body=%wide.region_12.16_spmd.sunk | while | flops 680460288 | bytes 40404820 | solution.py:244
  287.2 24.4 %while.58 = (s32[]{:T(128)}, f32[1024,128]{1,0:T(8,128)}, f32[1024,128]{1,0:T(8,128)}, bf16[2,512,128]{2,1,0:T(8,128)(2,1)}, s32[2]{0:T(128)S(1)}, /*index=5*/s3...) while((s32[]{:T(128)}, f32[1024,128]{1,0:T(8,128)}, ...), condition=%wide.region_15.15_spmd.clone, body=%wide.region_13.14_spmd.clone.sunk | while | flops 680198144 | bytes 27812304 | solution.py:109
  319.2 24.4 %while.58 = (s32[]{:T(128)}, f32[1024,128]{1,0:T(8,128)}, f32[1024,128]{1,0:T(8,128)}, bf16[2,512,128]{2,1,0:T(8,128)(2,1)}, s32[2]{0:T(128)S(1)}, /*index=5*/s3...) while((s32[]{:T(128)}, f32[1024,128]{1,0:T(8,128)}, ...), condition=%wide.region_15.15_spmd.clone, body=%wide.region_13.14_spmd.clone.sunk | while | flops 680198144 | bytes 27812304 | solution.py:109
  351.3 24.4 %while.58 = (s32[]{:T(128)}, f32[1024,128]{1,0:T(8,128)}, f32[1024,128]{1,0:T(8,128)}, bf16[2,512,128]{2,1,0:T(8,128)(2,1)}, s32[2]{0:T(128)S(1)}, /*index=5*/s3...) while((s32[]{:T(128)}, f32[1024,128]{1,0:T(8,128)}, ...), condition=%wide.region_15.15_spmd.clone, body=%wide.region_13.14_spmd.clone.sunk | while | flops 680198144 | bytes 27812304 | solution.py:109
  383.3 24.4 %while.58 = (s32[]{:T(128)}, f32[1024,128]{1,0:T(8,128)}, f32[1024,128]{1,0:T(8,128)}, bf16[2,512,128]{2,1,0:T(8,128)(2,1)}, s32[2]{0:T(128)S(1)}, /*index=5*/s3...) while((s32[]{:T(128)}, f32[1024,128]{1,0:T(8,128)}, ...), condition=%wide.region_15.15_spmd.clone, body=%wide.region_13.14_spmd.clone.sunk | while | flops 680198144 | bytes 27812304 | solution.py:109
  420.1 8.0 all-to-all-done.5
  433.4 7.6 all-to-all-done.6
  455.5 8.3 convolution_convert_fusion.3
  465.4 9.2 %convolution_convert_fusion.2 = bf16[1024,4096]{1,0:T(8,128)(2,1)} fusion(bf16[512,4096]{1,0:T(8,128)(2,1)} %get-tuple-element.419, f32[512,1024]{1,0:T(8,128)S(1)} %copy-done.9, f32[1024]{0:T(1024)S(1)} %copy-done.49, f32[1024]{0:T(1024)S(1)} %copy-done.35, f32[512]{0:T(512)S(1)} %copy-done.40, f32[512]{0:T(512)S(1)} %copy-done.27), kind=kOutput, calls=%fused_computation.63 | convolution fusion | flops 4301783040 | bytes 14692352 | tf_op jit(solution)/shard_map/dot_general | solution.py:207
  475.4 14.0 %convolution_convert_fusion.1 = bf16[4096,1024]{1,0:T(8,128)(2,1)} fusion(bf16[1,512,1024]{2,1,0:T(8,128)(2,1)} %param.39, f32[512,4096]{1,0:T(8,128)} %fusion.67, f32[4096]{0:T(1024)S(1)} %copy-done.38), kind=kOutput, calls=%fused_computation.62 | convolution fusion | flops 4320133120 | bytes 17842176 | tf_op jit(solution)/shard_map/dot_general | solution.py:199
  490.0 58.4 %reduce-scatter.9.cloned.1.call-done = bf16[64,3072]{1,0:T(8,128)(2,1)} async-done(((bf16[1024,3072]{1,0:T(8,128)(2,1)}), bf16[64,3072]{1,0:T(8,128)(2,1)}) %reduce-scatter.9.cloned.1.call-update) | async-done | bytes 393232 | tf_op jit(solution)/shard_map/reduce_scatter | solution.py:268
  548.5 12.2 %fusion.50 = bf16[1,512,1024]{2,1,0:T(8,128)(2,1)} fusion(f32[512,1024]{1,0:T(8,128)S(1)} %copy-done.9, bf16[4096,1024]{1,0:T(8,128)(2,1)} %param.37, f32[1024]{0:T(1024)S(1)} %convert_element_type.168, f32[512,4096]{1,0:T(8,128)} %fusion.67, f32[4096]{0:T(1024)S(1)} %copy-done.38), kind=kOutput, calls=%fused_computation.107 | convolution fusion | flops 4317511680 | bytes 19943424 | tf_op jit(solution)/shard_map/dot_general | solution.py:193
  560.7 95.6 %reduce-scatter.17.cloned.1.call-done = bf16[64,4096]{1,0:T(8,128)(2,1)} async-done(((bf16[1024,4096]{1,0:T(8,128)(2,1)}), bf16[64,4096]{1,0:T(8,128)(2,1)}) %reduce-scatter.17.cloned.1.call-update) | async-done | bytes 524304 | tf_op jit(solution)/shard_map/reduce_scatter | solution.py:274
  656.7 9.1 %fusion.44 = (f32[1024]{0:T(1024)S(1)}, f32[512]{0:T(512)S(1)}, f32[512]{0:T(512)S(1)}, f32[1024]{0:T(1024)S(1)}, f32[512,1024]{1,0:T(8,128)}) fusion(bf16[1,512,1024]{2,1,0:T(8,128)(2,1)S(1)} %copy-done.11, f32[512]{0:T(512)S(1)} %copy-done.43, f32[512]{0:T(512)S(1)} %copy-done.29, f32[1024]{0:T(1024)S(1)} %copy-done.33, bf16[1024,3072]{1,0:T(8,128)(2,1)} %param.26, ...), kind=kOutput, calls=%fused_computation.85 | convolution fusion | flops 3235902464 | bytes 12603392 | tf_op jit(solution)/shard_map/dot_general | solution.py:261
  665.8 98.8 %reduce-scatter.21.cloned.1.call-done = bf16[256,1024]{1,0:T(8,128)(2,1)} async-done(((bf16[4096,1024]{1,0:T(8,128)(2,1)}), bf16[256,1024]{1,0:T(8,128)(2,1)}) %reduce-scatter.21.cloned.1.call-update) | async-done | bytes 524304 | tf_op jit(solution)/shard_map/reduce_scatter | solution.py:277
  764.9 41.7 %all-reduce = (f32[1024]{0:T(1024)}, f32[1024]{0:T(1024)}, f32[1024]{0:T(1024)}, f32[1024]{0:T(1024)}, f32[1024]{0:T(1024)}, /*index=5*/f32[1024]{0:T(1024)}, f32[1024]{0:T(1024)}, f32[4096]{0:T(1024)}, f32[1024]{0:T(1024)}) all-reduce(f32[1024]{0:T(1024)S(1)} %bitcast.291, ...), channel_id=1, replica_groups=mesh['dp'=16,'seq'=2] {'dp','seq'}, use_global_device_ids=true, to_apply=%region_22.23 | all-reduce | flops 12288 | bytes 98304 | tf_op jit(solution)/shard_map/psum | solution.py:295
  816.1 10.1 %reduce-scatter.23.cloned.1.call-done = bf16[256,512]{1,0:T(8,128)(2,1)} async-done(((bf16[256,1024]{1,0:T(8,128)(2,1)}), bf16[256,512]{1,0:T(8,128)(2,1)}) %reduce-scatter.23.cloned.1.call-update) | async-done | bytes 262160 | tf_op jit(solution)/shard_map/reduce_scatter | solution.py:291
  (563 shorter events, 314.0 us)
Async XLA Ops:
  7.2 216.4 %copy-start = (bf16[1024,1024]{1,0:T(8,128)(2,1)S(1)}, bf16[1024,1024]{1,0:T(8,128)(2,1)}, u32[]{:S(2)}) copy-start(bf16[1024,1024]{1,0:T(8,128)(2,1)} %param.29) | copy-start | bytes 6291460
  20.5 19.6 %all-to-all-start = ((bf16[512,8,128]{2,0,1:T(8,128)(2,1)}), bf16[512,8,128]{2,0,1:T(8,128)(2,1)}, u32[]{:S(2)}, u32[]{:S(2)}) async-start(bf16[512,8,128]{2,0,1:T(8,128)(2,1)} %bitcast.263), calls=%async_computation | async-start | bytes 2097152 | tf_op jit(solution)/shard_map/all_to_all | solution.py:153
  40.1 17.9 %all-to-all-start.2 = ((bf16[512,8,128]{2,0,1:T(8,128)(2,1)}), bf16[512,8,128]{2,0,1:T(8,128)(2,1)}, u32[]{:S(2)}, u32[]{:S(2)}) async-start(bf16[512,8,128]{2,0,1:T(8,128)(2,1)} %bitcast.261), calls=%async_computation.2 | async-start | bytes 2097152 | tf_op jit(solution)/shard_map/all_to_all | solution.py:155
  58.0 21.6 %all-to-all-start.1 = ((bf16[512,8,128]{2,0,1:T(8,128)(2,1)}), bf16[512,8,128]{2,0,1:T(8,128)(2,1)}, u32[]{:S(2)}, u32[]{:S(2)}) async-start(bf16[512,8,128]{2,0,1:T(8,128)(2,1)} %copy_bitcast_fusion.2), calls=%async_computation.1 | async-start | bytes 2097152 | tf_op jit(solution)/shard_map/all_to_all | solution.py:154
  202.3 16.7 %all-to-all-start.3 = ((bf16[1024,4,128]{2,1,0:T(4,128)(2,1)}), bf16[1024,4,128]{2,1,0:T(4,128)(2,1)}, u32[]{:S(2)}, u32[]{:S(2)}) async-start(bf16[1024,4,128]{2,1,0:T(4,128)(2,1)} %bitcast.262), calls=%async_computation.3 | async-start | bytes 2097152 | tf_op jit(solution)/shard_map/all_to_all | solution.py:175
  207.3 54.1 %copy-start.34 = (f32[1024]{0:T(1024)}, f32[1024]{0:T(1024)S(1)}, u32[]{:S(2)}) copy-start(f32[1024]{0:T(1024)S(1)} %convert_element_type.163) | copy-start | bytes 12292
  207.4 19.2 %copy-start.48 = (f32[1024]{0:T(1024)}, f32[1024]{0:T(1024)S(1)}, u32[]{:S(2)}) copy-start(f32[1024]{0:T(1024)S(1)} %convert_element_type.164) | copy-start | bytes 12292
  207.4 30.0 %copy-start.37 = (f32[4096]{0:T(1024)}, f32[4096]{0:T(1024)S(1)}, u32[]{:S(2)}) copy-start(f32[4096]{0:T(1024)S(1)} %convert_element_type.166) | copy-start | bytes 49156
  226.2 35.2 %copy-start.8 = (f32[512,1024]{1,0:T(8,128)}, f32[512,1024]{1,0:T(8,128)S(1)}, u32[]{:S(2)}) copy-start(f32[512,1024]{1,0:T(8,128)S(1)} %get-tuple-element.415) | copy-start | bytes 6291460
  226.2 35.2 %copy-start.26 = (f32[512]{0:T(512)}, f32[512]{0:T(512)S(1)}, u32[]{:S(2)}) copy-start(f32[512]{0:T(512)S(1)} %broadcast_multiply_fusion.4) | copy-start | bytes 6148
  226.6 34.8 %copy-start.39 = (f32[512]{0:T(512)}, f32[512]{0:T(512)S(1)}, u32[]{:S(2)}) copy-start(f32[512]{0:T(512)S(1)} %add_rsqrt_fusion) | copy-start | bytes 6148
  226.6 27.0 %slice-start = ((s8[8388608]{0:T(1024)(128)(4,1)}), s8[4194304]{0:T(1024)(128)(4,1)S(1)}, s32[]{:S(2)}) async-start(s8[8388608]{0:T(1024)(128)(4,1)} %bitcast.293), calls=%async_computation.24 | async-start | bytes 8388608
  265.5 14.5 %all-to-all-start.4 = ((bf16[512,8,128]{2,0,1:T(8,128)(2,1)}), bf16[512,8,128]{2,0,1:T(8,128)(2,1)S(1)}, u32[]{:S(2)}, u32[]{:S(2)}) async-start(bf16[512,8,128]{2,0,1:T(8,128)(2,1)} %bitcast.260), calls=%async_computation.4 | async-start | bytes 2097152 | tf_op jit(solution)/shard_map/all_to_all | solution.py:223
  269.2 220.2 %reduce-scatter.13.cloned.1.call-start = ((), (), s32[]{:S(2)}) async-start(), calls=%async_computation.18 | async-start | bytes 2228224 | tf_op jit(solution)/shard_map/reduce_scatter | solution.py:271
  414.7 13.4 %all-to-all-start.5 = ((bf16[1024,4,128]{2,1,0:T(4,128)(2,1)}), bf16[1024,4,128]{2,1,0:T(4,128)(2,1)S(1)}, u32[]{:S(2)}, u32[]{:S(2)}) async-start(bf16[1024,4,128]{2,1,0:T(4,128)(2,1)} %bitcast.193), calls=%async_computation.5 | async-start | bytes 2097152 | tf_op jit(solution)/shard_map/all_to_all | solution.py:248
  428.1 13.0 %all-to-all-start.6 = ((bf16[1024,4,128]{2,1,0:T(4,128)(2,1)}), bf16[1024,4,128]{2,1,0:T(4,128)(2,1)S(1)}, u32[]{:S(2)}, u32[]{:S(2)}) async-start(bf16[1024,4,128]{2,1,0:T(4,128)(2,1)} %bitcast.192), calls=%async_computation.6 | async-start | bytes 2097152 | tf_op jit(solution)/shard_map/all_to_all | solution.py:249
  441.0 13.0 %all-to-all-start.7 = ((bf16[1024,4,128]{2,1,0:T(4,128)(2,1)}), bf16[1024,4,128]{2,1,0:T(4,128)(2,1)S(1)}, u32[]{:S(2)}, u32[]{:S(2)}) async-start(bf16[1024,4,128]{2,1,0:T(4,128)(2,1)} %bitcast.259), calls=%async_computation.7 | async-start | bytes 2097152 | tf_op jit(solution)/shard_map/all_to_all | solution.py:250
  444.6 103.8 %reduce-scatter.9.cloned.1.call-start = ((), (), s32[]{:S(2)}) async-start(), calls=%async_computation.16 | async-start | bytes 6684672 | tf_op jit(solution)/shard_map/reduce_scatter | solution.py:268
  463.9 192.4 %reduce-scatter.17.cloned.1.call-start = ((), (), s32[]{:S(2)}) async-start(), calls=%async_computation.20 | async-start | bytes 8912896 | tf_op jit(solution)/shard_map/reduce_scatter | solution.py:274
  474.7 289.9 %reduce-scatter.21.cloned.1.call-start = ((), (), s32[]{:S(2)}) async-start(), calls=%async_computation.22 | async-start | bytes 8912896 | tf_op jit(solution)/shard_map/reduce_scatter | solution.py:277
  489.4 321.7 %reduce-scatter.15.cloned.1.call-start = ((), (), s32[]{:S(2)}) async-start(), calls=%async_computation.19 | async-start | bytes 196608 | tf_op jit(solution)/shard_map/reduce_scatter | solution.py:285
  490.0 322.6 %reduce-scatter.11.cloned.1.call-start = ((), (), s32[]{:S(2)}) async-start(), calls=%async_computation.17 | async-start | bytes 589824 | tf_op jit(solution)/shard_map/reduce_scatter | solution.py:282
  548.4 265.9 %reduce-scatter.19.cloned.1.call-start = ((), (), s32[]{:S(2)}) async-start(), calls=%async_computation.21 | async-start | bytes 786432 | tf_op jit(solution)/shard_map/reduce_scatter | solution.py:288
  656.3 108.3 %copy-start.13 = (bf16[1024,4,128]{2,1,0:T(4,128)(2,1)S(1)}, bf16[1024,4,128]{2,1,0:T(4,128)(2,1)}, u32[]{:S(2)}) copy-start(bf16[1024,4,128]{2,1,0:T(4,128)(2,1)} %copy-done.12) | copy-start | bytes 3145732
  656.3 169.9 %reduce-scatter.23.cloned.1.call-start = ((), (), s32[]{:S(2)}) async-start(), calls=%async_computation.23 | async-start | bytes 786432 | tf_op jit(solution)/shard_map/reduce_scatter | solution.py:291
  665.7 99.0 %copy-start.15 = (bf16[1024,4,128]{2,1,0:T(4,128)(2,1)S(1)}, bf16[1024,4,128]{2,1,0:T(4,128)(2,1)}, u32[]{:S(2)}) copy-start(bf16[1024,4,128]{2,1,0:T(4,128)(2,1)} %copy-done.14) | copy-start | bytes 3145732
  665.7 99.1 %copy-start.30 = (f32[1024]{0:T(1024)S(1)}, f32[1024]{0:T(1024)}, u32[]{:S(2)}) copy-start(f32[1024]{0:T(1024)} %get-tuple-element.401) | copy-start | bytes 12292
  665.7 99.1 %copy-start.31 = (f32[1024]{0:T(1024)S(1)}, f32[1024]{0:T(1024)}, u32[]{:S(2)}) copy-start(f32[1024]{0:T(1024)} %get-tuple-element.413) | copy-start | bytes 12292
  665.7 99.1 %copy-start.36 = (f32[4096]{0:T(1024)S(1)}, f32[4096]{0:T(1024)}, u32[]{:S(2)}) copy-start(f32[4096]{0:T(1024)} %get-tuple-element.418) | copy-start | bytes 49156
  665.7 99.1 %copy-start.44 = (f32[1024]{0:T(1024)S(1)}, f32[1024]{0:T(1024)}, u32[]{:S(2)}) copy-start(f32[1024]{0:T(1024)} %get-tuple-element.296) | copy-start | bytes 12292
  665.8 99.1 %copy-start.45 = (f32[1024]{0:T(1024)S(1)}, f32[1024]{0:T(1024)}, u32[]{:S(2)}) copy-start(f32[1024]{0:T(1024)} %get-tuple-element.302) | copy-start | bytes 12292
  806.7 21.4 %copy-start.1 = (bf16[1024,1024]{1,0:T(8,128)(2,1)S(1)}, bf16[1024,1024]{1,0:T(8,128)(2,1)}, u32[]{:S(2)}) copy-start(bf16[1024,1024]{1,0:T(8,128)(2,1)} %param.29) | copy-start | bytes 6291460
  (107 other events, 456.3 us)
Sparse Core Ops, SparseCore 0:
  273.8 62.6 reduce-scatter.12
  464.0 84.3 reduce-scatter.8
  552.5 103.7 reduce-scatter.16
  660.2 104.3 reduce-scatter.20
  766.7 10.0 reduce-scatter.14
  778.8 13.2 reduce-scatter.10
  794.4 15.0 reduce-scatter.18
  811.8 14.3 reduce-scatter.22
where the time goes:
time: 845 us; the launch traced here: 835 us
  waiting for transfers between devices  325 us (38%)
  matrix products  214 us (25%)
  local copies, waits for them, and re-layouts  104 us (12%)
  other arithmetic  56.2 us (7%)
  blocking collectives  54.2 us (6%)
  starting transfers between devices  33.6 us (4%)
  loops' own time  33 us (4%)
  between operations  15.4 us (2%)
    reduce_scatter x1, waiting for transfers between devices, local(): lax.psum_scatter(matrices[3].astype(jnp.bfloat16), 'dp', scatter_dimensio...  98.8 us
    reduce_scatter x1, waiting for transfers between devices, local(): lax.psum_scatter(matrices[2].astype(jnp.bfloat16), 'dp', scatter_dimensio...  95.6 us
    reduce_scatter x1, waiting for transfers between devices, local(): lax.psum_scatter(matrices[0].astype(jnp.bfloat16), 'dp', scatter_dimensio...  58.4 us
    dot_general x16, matrix products, block_scores(): lax.dot_general(query_block, key_rows, (((1,), (1,)), ((), ())), preferre...  45.7 us
    psum x1, blocking collectives, local(): lax.psum((g_bias_q, g_bias_v, g_bias_out, g_gain_one, g_shift_one, g_gain...  41.7 us
    squeeze x24, local copies, waits for them, and re-layouts, local(): lax.map(forward_head, (head_q, head_k, head_v, slopes))  23.8 us
    dot_general x8, matrix products, one_block(): jnp.dot(weights, value_rows, preferred_element_type=jnp.float32)  22.3 us
    dot_general x8, matrix products, one_block(): lax.dot_general(weights.astype(jnp.bfloat16), grad_block, (((0,), (0,)),...  18.8 us
  transfers between devices with their start and end apart: 16, of which 11 were waited for; matrix products, arithmetic and copies ran while one was open for 24% of the time, Pallas kernels for 0%

commit v1 on v0

--- a/solution.py
+++ b/solution.py
@@ -1,13 +1,789 @@
+import functools
+
 import jax
 import jax.numpy as jnp
+import numpy as np
 from jax import lax
+from jax.experimental import pallas as pl
+from jax.experimental.pallas import tpu as pltpu
 from jax.sharding import PartitionSpec as P
 
 HEAD_DIM = 128
-
+MESH = pl.DeviceIdType.MESH
+F32 = jnp.float32
+BF16 = jnp.bfloat16
+LOG2E = 1.4426950408889634
+FAR = 1e30
+GELU_C = 0.7978845608028654
+GELU_A = 0.044715
 
 norm_eps = 1e-05
 masked_score = -1e30
+
+NT = (((1,), (1,)), ((), ()))
+TN = (((0,), (0,)), ((), ()))
+
+
+def dot(a, b):
+    return jnp.dot(a, b, preferred_element_type=F32)
+
+
+def dot_nt(a, b):
+    return lax.dot_general(a, b, NT, preferred_element_type=F32)
+
+
+def dot_tn(a, b):
+    return lax.dot_general(a, b, TN, preferred_element_type=F32)
+
+
+def coords():
+    dp = lax.axis_index("dp")
+    return {
+        "c": dp % 2,
+        "x": (dp // 2) % 2,
+        "a": (dp // 4) % 2,
+        "b": dp // 8,
+        "y": lax.axis_index("seq"),
+    }
+
+
+def partner(kind):
+    dp = lax.axis_index("dp")
+    if kind == "y":
+        return {"seq": 1 - lax.axis_index("seq")}
+    step = {"c": 1, "x": 2, "a": 4, "b": 8}[kind]
+    bit = (dp // step) % 2
+    return {"dp": dp + step - 2 * step * bit}
+
+
+def greet(kinds):
+    barrier = pltpu.get_barrier_semaphore()
+    for kind in kinds:
+        pl.semaphore_signal(barrier, inc=1, device_id=partner(kind), device_id_type=MESH)
+    pl.semaphore_wait(barrier, len(kinds))
+
+
+ORDERS = (("x", "a", "y", "b"), ("y", "a", "x", "b"))
+
+
+def block_index(half, place):
+    index = half * 16
+    for kind, weight in zip(ORDERS[half], (8, 4, 2, 1)):
+        index = index + place[kind] * weight
+    return index
+
+
+def dp_bits(dp):
+    return {"c": dp % 2, "x": (dp // 2) % 2, "a": (dp // 4) % 2, "b": dp // 8}
+
+
+class Scatter:
+    def __init__(self, held, arrivals, send_sem, recv_sem):
+        self.held, self.arrivals = held, arrivals
+        self.send_sem, self.recv_sem = send_sem, recv_sem
+        self.me = coords()
+
+    def offset(self, half, stage, other):
+        index = half * 16
+        for k, weight in zip(range(stage + 1), (8, 4, 2, 1)):
+            bit = self.me[ORDERS[half][k]]
+            if other and k == stage:
+                bit = 1 - bit
+            index = index + bit * weight
+        return index
+
+    def copy(self, chunk, stage, half):
+        size = 8 >> stage
+        return pltpu.make_async_remote_copy(
+            src_ref=self.held.at[chunk, pl.ds(self.offset(half, stage, True), size)],
+            dst_ref=self.arrivals[stage].at[chunk, half],
+            send_sem=self.send_sem.at[stage, chunk, half],
+            recv_sem=self.recv_sem.at[stage, chunk, half],
+            device_id=partner(ORDERS[half][stage]),
+            device_id_type=MESH,
+        )
+
+    def start(self, chunk, stage):
+        for half in range(2):
+            self.copy(chunk, stage, half).start()
+
+    def finish(self, chunk, stage):
+        size = 8 >> stage
+        for half in range(2):
+            self.copy(chunk, stage, half).wait()
+            mine = pl.ds(self.offset(half, stage, False), size)
+            self.held[chunk, mine] = self.held[chunk, mine] + self.arrivals[stage][chunk, half]
+
+    def result(self, chunk, half):
+        return self.held[chunk, self.offset(half, 3, False)].astype(F32)
+
+
+def arrival_shapes(chunks):
+    return [pltpu.VMEM((chunks, 2, 8 >> k, 32, 256), BF16) for k in range(4)]
+
+
+def when(cond, fn):
+    if isinstance(cond, (bool, np.bool_)):
+        if cond:
+            fn()
+    else:
+        pl.when(cond)(fn)
+
+
+def inside(value, low, high):
+    if isinstance(value, int):
+        return low <= value < high
+    return (value >= low) & (value < high)
+
+
+def kernel_one(
+    halo, x_ref, doc_ref, slope_ref, bq_ref, bv_ref, bo_ref, g1_ref, s1_ref, g2_ref, s2_ref, wqkv_hbm, wout_hbm,
+    act2_hbm, act2t_hbm, x2_hbm, qkv_hbm, ot_hbm, act1t_hbm, dist_hbm,
+    act1, act1t, qkv, o_s, ot, act2, act2t, x2, dist, xh, doch, bias, wqkv, wout,
+    wsem, osem, hs, hr,
+):
+    tokens, width = x_ref.shape
+    heads = width // HEAD_DIM
+    ext = tokens + halo
+    seq = lax.axis_index("seq")
+
+    wcopies = [
+        pltpu.make_async_copy(
+            wqkv_hbm.at[:, pl.ds(j * 512, 512)], wqkv.at[:, pl.ds(j * 512, 512)], wsem.at[j]
+        )
+        for j in range(6)
+    ]
+    wcopies.append(pltpu.make_async_copy(wout_hbm, wout, wsem.at[6]))
+    for cp in wcopies:
+        cp.start()
+    greet(("y",))
+    send_x = pltpu.make_async_remote_copy(
+        src_ref=x_ref.at[pl.ds(tokens - halo, halo)], dst_ref=xh, send_sem=hs.at[0], recv_sem=hr.at[0],
+        device_id=partner("y"), device_id_type=MESH,
+    )
+    send_doc = pltpu.make_async_remote_copy(
+        src_ref=doc_ref, dst_ref=doch, send_sem=hs.at[1], recv_sem=hr.at[1],
+        device_id=partner("y"), device_id_type=MESH,
+    )
+
+    @pl.when(seq == 0)
+    def _():
+        send_doc.start()
+        send_x.start()
+
+    gain1, shift1 = g1_ref[...].astype(F32), s1_ref[...].astype(F32)
+    gain2, shift2 = g2_ref[...].astype(F32), s2_ref[...].astype(F32)
+
+    def norm(v, gain, shift):
+        center = v - jnp.mean(v, axis=-1, keepdims=True)
+        inv = lax.rsqrt(jnp.mean(center * center, axis=-1, keepdims=True) + norm_eps)
+        return center * inv * gain + shift
+
+    bias[:, 0:width] = bq_ref[...].astype(F32)
+    bias[:, width : 2 * width] = jnp.zeros((1, width), F32)
+    bias[:, 2 * width :] = bv_ref[...].astype(F32)
+
+    for r in range(tokens // 128):
+        v = norm(x_ref[r * 128 : (r + 1) * 128].astype(F32), gain1, shift1).astype(BF16)
+        act1[halo + r * 128 : halo + (r + 1) * 128] = v
+        act1t[:, halo + r * 128 : halo + (r + 1) * 128] = v.T
+
+    for j in range(6):
+        wcopies[j].wait()
+        cols = slice(j * 512, (j + 1) * 512)
+        for m in range(tokens // 256):
+            rows = slice(halo + m * 256, halo + (m + 1) * 256)
+            qkv[rows, cols] = (dot(act1[rows], wqkv[:, cols]) + bias[:, cols]).astype(BF16)
+
+    def distances(block):
+        keys = doch_ext[block * 256 : block * 256 + 512]
+        queries = doc_rows[:, block * 256 : block * 256 + 256]
+        key_pos = lax.broadcasted_iota(jnp.int32, (512, 256), 0)
+        query_pos = lax.broadcasted_iota(jnp.int32, (512, 256), 1) + 256
+        gap = query_pos - key_pos
+        allowed = (gap >= 0) & (keys == queries)
+        dist[block] = jnp.where(allowed, gap.astype(F32), FAR)
+
+    own_doc = doc_ref[...].astype(F32)[0:1]
+    doc_rows = own_doc
+    own_cols = jnp.transpose(jnp.broadcast_to(own_doc, (128, tokens)))[:, 0:1]
+
+    def attend(block):
+        def one_head(h, carry):
+            c0 = pl.multiple_of(h * HEAD_DIM, HEAD_DIM)
+            q = qkv[halo + block * 256 : halo + (block + 1) * 256, pl.ds(c0, HEAD_DIM)]
+            k = qkv[block * 256 : block * 256 + 512, pl.ds(width + c0, HEAD_DIM)]
+            v = qkv[block * 256 : block * 256 + 512, pl.ds(2 * width + c0, HEAD_DIM)]
+            slope = slope_ref[pl.ds(h, 1), 0:1]
+            s = dot_nt(k, q) * (LOG2E * HEAD_DIM**-0.5) - slope * dist[block]
+            e = jnp.exp2(s - jnp.max(s, axis=0, keepdims=True))
+            p = (e * (1.0 / jnp.sum(e, axis=0, keepdims=True))).astype(BF16)
+            o_t = dot_tn(v, p)
+            ot[pl.ds(c0, HEAD_DIM), block * 256 : (block + 1) * 256] = o_t.astype(BF16)
+            o_s[block * 256 : (block + 1) * 256, pl.ds(c0, HEAD_DIM)] = o_t.T.astype(BF16)
+            return carry
+
+        lax.fori_loop(0, heads, one_head, 0)
+
+    def project(block):
+        for r in range(2):
+            rows = slice(block * 256 + r * 128, block * 256 + (r + 1) * 128)
+            second = x_ref[rows].astype(F32) + dot(o_s[rows], wout[...]) + bo_ref[...].astype(F32)
+            x2[rows] = second
+            v = norm(second, gain2, shift2).astype(BF16)
+            act2[rows] = v
+            act2t[:, rows] = v.T
+
+    doch_ext = jnp.concatenate([jnp.full((halo, 1), -1.0, F32), own_cols], axis=0)
+    distances(1)
+    attend(1)
+    wcopies[6].wait()
+    project(1)
+
+    @pl.when(seq == 0)
+    def _():
+        send_doc.wait_send()
+        send_x.wait_send()
+        doch[...] = jnp.full(doch.shape, -1, jnp.int32)
+        xh[...] = jnp.zeros(xh.shape, BF16)
+        act1[0:halo] = jnp.zeros((halo, width), BF16)
+        act1t[:, 0:halo] = jnp.zeros((width, halo), BF16)
+        qkv[0:halo] = jnp.zeros((halo, 3 * width), BF16)
+
+    @pl.when(seq == 1)
+    def _():
+        send_doc.wait_recv()
+        send_x.wait_recv()
+        for r in range(halo // 128):
+            v = norm(xh[r * 128 : (r + 1) * 128].astype(F32), gain1, shift1).astype(BF16)
+            act1[r * 128 : (r + 1) * 128] = v
+            act1t[:, r * 128 : (r + 1) * 128] = v.T
+        for j in range(2, 6):
+            cols = slice(j * 512, (j + 1) * 512)
+            qkv[0:halo, cols] = (dot(act1[0:halo], wqkv[:, cols]) + bias[:, cols]).astype(BF16)
+
+    halo_doc = doch[...].astype(F32)[0:1, tokens - halo :]
+    halo_cols = jnp.transpose(jnp.broadcast_to(halo_doc, (128, halo)))[:, 0:1]
+    doch_ext = jnp.concatenate([halo_cols, own_cols], axis=0)
+    distances(0)
+    attend(0)
+    project(0)
+    outs = [
+        pltpu.make_async_copy(s, d, osem.at[i])
+        for i, (s, d) in enumerate(
+            (
+                (act2, act2_hbm), (act2t, act2t_hbm), (x2, x2_hbm), (qkv, qkv_hbm), (ot, ot_hbm),
+                (act1t, act1t_hbm), (dist, dist_hbm),
+            )
+        )
+    ]
+    for cp in outs:
+        cp.start()
+    for cp in outs:
+        cp.wait()
+
+
+def kernel_two(
+    act2, act2t, cot, x2, g2_ref, bup_ref, bdown_ref, wup_hbm, wdown_hbm,
+    out, gwu, dx2, ab, hd_hbm, vec,
+    hid_t, hid, dpre, dn2, outacc, wu, wd, grad, came, held, r1, r2, r3, r4, gradd, camed,
+    wsem, cs, cr, ss, rs, dcs, dcr, dsem,
+):
+    tokens, width = act2.shape
+    ff = wup_hbm.shape[1]
+    half = ff // 2
+    steps = half // 256
+    me = coords()
+
+    def weights(f, slot):
+        col = pl.multiple_of(f * 256, 256)
+        return [
+            pltpu.make_async_copy(wup_hbm.at[:, pl.ds(col, 256)], wu.at[slot, :, pl.ds(0, 256)], wsem.at[slot, 0]),
+            pltpu.make_async_copy(
+                wup_hbm.at[:, pl.ds(half + col, 256)], wu.at[slot, :, pl.ds(256, 256)], wsem.at[slot, 1]
+            ),
+            pltpu.make_async_copy(wdown_hbm.at[pl.ds(col, 256)], wd.at[slot, pl.ds(0, 256)], wsem.at[slot, 2]),
+            pltpu.make_async_copy(
+                wdown_hbm.at[pl.ds(half + col, 256)], wd.at[slot, pl.ds(256, 256)], wsem.at[slot, 3]
+            ),
+        ]
+
+    for cp in weights(0, 0):
+        cp.start()
+    greet(("c", "x", "a", "b", "y"))
+    scatter = Scatter(held, (r1, r2, r3, r4), ss, rs)
+
+    def core_copy(f):
+        slot = f % 2
+        return pltpu.make_async_remote_copy(
+            src_ref=grad.at[slot, 1 - me["c"]], dst_ref=came.at[f], send_sem=cs.at[slot], recv_sem=cr.at[f],
+            device_id=partner("c"), device_id_type=MESH,
+        )
+
+    def finish_core(f):
+        core_copy(f).wait()
+        held[f] = grad[f % 2, me["c"]] + came[f]
+        scatter.start(f, 0)
+
+    def event(t):
+        def last():
+            scatter.finish(t - 5, 3)
+            for h in range(2):
+                gwu[pl.ds(h * 32, 32), pl.ds(pl.multiple_of((t - 5) * 256, 256), 256)] = scatter.result(t - 5, h)
+
+        when(inside(t, 5, steps + 5), last)
+        for stage in (2, 1, 0):
+            lag = stage + 2
+
+            def step(stage=stage, lag=lag):
+                scatter.finish(t - lag, stage)
+                scatter.start(t - lag, stage + 1)
+
+            when(inside(t, lag, steps + lag), step)
+        when(inside(t, 1, steps + 1), lambda: finish_core(t - 1))
+
+    vec[...] = jnp.zeros(vec.shape, F32)
+    vec[7:8] = jnp.sum(cot[...].astype(F32), axis=0, keepdims=True)
+    dn2[...] = jnp.zeros(dn2.shape, F32)
+    outacc[...] = x2[...] + bdown_ref[...].astype(F32)
+
+    def body(f, carry):
+        slot = f % 2
+        for cp in weights(f, slot):
+            cp.wait()
+
+        @pl.when(f + 1 < steps)
+        def _():
+            for cp in weights(f + 1, 1 - slot):
+                cp.start()
+
+        event(f)
+        for yy in range(2):
+            cols = slice(yy * 256, (yy + 1) * 256)
+            first = pl.multiple_of(yy * half + f * 256, 256)
+            bias = bup_ref[:, pl.ds(first, 256)].astype(F32)
+            sums = jnp.zeros((1, 256), F32)
+            for m in range(tokens // 256):
+                rows = slice(m * 256, (m + 1) * 256)
+                u = dot(act2[rows], wu[slot, :, cols]) + bias
+                dh = dot_nt(cot[rows], wd[slot, cols])
+                uu = u * u
+                th = jnp.tanh(GELU_C * u * (1.0 + GELU_A * uu))
+                half_u = 0.5 * u
+                hv = (half_u * (1.0 + th)).astype(BF16)
+                slope = 0.5 * (1.0 + th) + half_u * (1.0 - th * th) * (GELU_C * (1.0 + 3.0 * GELU_A * uu))
+                dv = (dh * slope).astype(BF16)
+                hid[rows, cols] = hv
+                dpre[rows, cols] = dv
+                hid_t[pl.ds(first, 256), rows] = hv.T
+                sums = sums + jnp.sum(dv.astype(F32), axis=0, keepdims=True)
+            row = yy * (half // width) + f // (width // 256)
+            vec[pl.ds(8 + row, 1), pl.ds(pl.multiple_of((f % (width // 256)) * 256, 256), 256)] = sums
+        for yy in range(2):
+            cols = slice(yy * 256, (yy + 1) * 256)
+            for m in range(width // 256):
+                tile = dot(act2t[m * 256 : (m + 1) * 256], dpre[:, cols])
+                for q in range(4):
+                    place = dp_bits(m * 4 + q)
+                    place["y"] = yy
+                    for h in range(2):
+                        r0 = q * 64 + h * 32
+                        grad[slot, place["c"], block_index(h, place)] = tile[r0 : r0 + 32].astype(BF16)
+        core_copy(f).start()
+        for m in range(tokens // 256):
+            rows = slice(m * 256, (m + 1) * 256)
+            dn2[rows] += dot_nt(dpre[rows], wu[slot])
+            outacc[rows] += dot(hid[rows], wd[slot])
+        return carry
+
+    lax.fori_loop(0, steps, body, 0)
+    out[...] = outacc[...].astype(BF16)
+
+    def down_copy(kk):
+        return pltpu.make_async_remote_copy(
+            src_ref=gradd.at[kk, 1 - me["c"]], dst_ref=camed.at[kk], send_sem=dcs.at[kk], recv_sem=dcr.at[kk],
+            device_id=partner("c"), device_id_type=MESH,
+        )
+
+    for kk in range(2):
+        for yy in range(2):
+            event(steps + kk * 2 + yy)
+
+            def tiles(m, carry, kk=kk, yy=yy):
+                tile = dot(hid_t[pl.ds(pl.multiple_of(m * 256, 256), 256)], cot[:, yy * 512 + kk * 256 : yy * 512 + kk * 256 + 256])
+                place = dp_bits(m)
+                place["y"] = yy
+                for rr in range(4):
+                    for h in range(2):
+                        r0 = rr * 64 + h * 32
+                        gradd[kk, place["c"], rr, block_index(h, place)] = tile[r0 : r0 + 32].astype(BF16)
+                return carry
+
+            lax.fori_loop(0, 16, tiles, 0)
+        down_copy(kk).start()
+
+    gain2 = g2_ref[...].astype(F32)
+
+    def norm_rows(r, carry):
+        rows = pl.ds(pl.multiple_of(r * 64, 64), 64)
+        v = x2[rows]
+        center = v - jnp.mean(v, axis=-1, keepdims=True)
+        inv = lax.rsqrt(jnp.mean(center * center, axis=-1, keepdims=True) + norm_eps)
+        normed = center * inv
+        dn = dn2[rows]
+        e = dn * gain2
+        vec[5:6] += jnp.sum(dn * normed, axis=0, keepdims=True)
+        vec[6:7] += jnp.sum(dn, axis=0, keepdims=True)
+        dx = cot[rows].astype(F32) + inv * (
+            e - jnp.mean(e, axis=-1, keepdims=True) - normed * jnp.mean(e * normed, axis=-1, keepdims=True)
+        )
+        dx2[rows] = dx
+        low = dx.astype(BF16)
+        ab[rows] = low
+        vec[2:3] += jnp.sum(low.astype(F32), axis=0, keepdims=True)
+        return carry
+
+    lax.fori_loop(0, tokens // 64, norm_rows, 0)
+    event(steps + 4)
+    stores = []
+    for kk in range(2):
+        down_copy(kk).wait()
+
+        def add(rr, carry, kk=kk):
+            gradd[kk, me["c"], rr] = gradd[kk, me["c"], rr] + camed[kk, rr]
+            return carry
+
+        lax.fori_loop(0, 4, add, 0)
+        cp = pltpu.make_async_copy(gradd.at[kk, me["c"]], hd_hbm.at[pl.ds(kk * 4, 4)], dsem.at[kk])
+        cp.start()
+        stores.append(cp)
+    for cp in stores:
+        cp.wait()
+
+
+CHUNKS = 16
+
+
+def kernel_three(
+    halo, x_ref, slope_ref, g1_ref, ab, dx2, qkv, ot, act1t, dist, vec_in, hd_hbm, wqkv_hbm, wout_hbm,
+    gin, gwd, gwo, gwqkv, vec,
+    do, dqkv, dn1, dnh, dnc, wbuf, wout, grad, came, held, r1, r2, r3, r4, vin,
+    wsem, cs, cr, ss, rs, hsem, hs, hr, vs, vr,
+):
+    tokens, width = ab.shape
+    heads = width // HEAD_DIM
+    seq = lax.axis_index("seq")
+    me = coords()
+    load_down = pltpu.make_async_copy(hd_hbm, held.at[pl.ds(0, 8)], hsem.at[0])
+    load_down.start()
+    load_out = pltpu.make_async_copy(wout_hbm, wout, wsem.at[2])
+    load_out.start()
+    greet(("c", "x", "a", "b", "y"))
+    scatter = Scatter(held, (r1, r2, r3, r4), ss, rs)
+
+    def core_copy(t):
+        slot = (t - 8) % 8
+        return pltpu.make_async_remote_copy(
+            src_ref=grad.at[slot, 1 - me["c"]], dst_ref=came.at[slot], send_sem=cs.at[slot], recv_sem=cr.at[slot],
+            device_id=partner("c"), device_id_type=MESH,
+        )
+
+    def begin(t):
+        if t >= 8:
+            core_copy(t).wait()
+            held[t] = grad[t - 8, me["c"]] + came[t - 8]
+        scatter.start(t, 0)
+
+    def event(t):
+        if 4 <= t < CHUNKS + 4:
+            n = t - 4
+            scatter.finish(n, 3)
+            for h in range(2):
+                block = scatter.result(n, h)
+                if n < 8:
+                    gwd[(n % 4) * 64 + h * 32 : (n % 4) * 64 + h * 32 + 32, (n // 4) * 256 : (n // 4) * 256 + 256] = block
+                elif n < 10:
+                    gwo[h * 32 : h * 32 + 32, (n - 8) * 256 : (n - 8) * 256 + 256] = block
+                else:
+                    gwqkv[h * 32 : h * 32 + 32, (n - 10) * 256 : (n - 10) * 256 + 256] = block
+        for stage in (2, 1, 0):
+            n = t - stage - 1
+            if 0 <= n < CHUNKS:
+                scatter.finish(n, stage)
+                scatter.start(n, stage + 1)
+        if t + 1 < CHUNKS:
+            begin(t + 1)
+
+    load_down.wait()
+    begin(0)
+    event(0)
+
+    def put(slot, yy, m, tile):
+        for q in range(4):
+            place = dp_bits(m * 4 + q)
+            place["y"] = yy
+            for h in range(2):
+                r0 = q * 64 + h * 32
+                grad[slot, place["c"], block_index(h, place)] = tile[r0 : r0 + 32].astype(BF16)
+
+    for j in range(2):
+        for yy in range(2):
+            c0 = yy * 512 + j * 256
+            for m in range(width // 256):
+                put(j, yy, m, dot(ot[m * 256 : (m + 1) * 256], ab[:, c0 : c0 + 256]))
+        core_copy(8 + j).start()
+    load_out.wait()
+    for m in range(tokens // 256):
+        rows = slice(m * 256, (m + 1) * 256)
+        do[rows] = dot_nt(ab[rows], wout[...]).astype(BF16)
+    event(1)
+
+    scale = HEAD_DIM**-0.5
+    dqkv[0:halo, 0:width] = jnp.zeros((halo, width), BF16)
+    vec[...] = vec_in[...]
+
+    def one_head(h, carry):
+        c0 = pl.multiple_of(h * HEAD_DIM, HEAD_DIM)
+        slope = slope_ref[pl.ds(h, 1), 0:1]
+        parts = []
+        for block in range(2):
+            rows = slice(halo + block * 256, halo + (block + 1) * 256)
+            krows = slice(block * 256, block * 256 + 512)
+            q = qkv[rows, pl.ds(c0, HEAD_DIM)]
+            k = qkv[krows, pl.ds(width + c0, HEAD_DIM)]
+            v = qkv[krows, pl.ds(2 * width + c0, HEAD_DIM)]
+            g = do[block * 256 : (block + 1) * 256, pl.ds(c0, HEAD_DIM)]
+            s = dot_nt(k, q) * (LOG2E * scale) - slope * dist[block]
+            e = jnp.exp2(s - jnp.max(s, axis=0, keepdims=True))
+            p = e * (1.0 / jnp.sum(e, axis=0, keepdims=True))
+            dp = dot_nt(v, g)
+            delta = jnp.sum(p * dp, axis=0, keepdims=True)
+            ds = (p * (dp - delta)).astype(BF16)
+            dq = (dot_tn(ds, k) * scale).astype(BF16)
+            dqkv[rows, pl.ds(c0, HEAD_DIM)] = dq
+            dk = dot(ds, q) * scale
+            dv = dot(p.astype(BF16), g)
+            parts.append((dk, dv))
+        for which in range(2):
+            cols = pl.ds((1 + which) * width + c0, HEAD_DIM)
+            first, second = parts[0][which], parts[1][which]
+            dqkv[0:256, cols] = first[0:256].astype(BF16)
+            dqkv[256:512, cols] = (first[256:512] + second[0:256]).astype(BF16)
+            dqkv[512:768, cols] = second[256:512].astype(BF16)
+        return carry
+
+    for group in range(4):
+        lax.fori_loop(group * 2, group * 2 + 2, one_head, 0)
+        event(2 + group)
+
+    vec[0:1] = jnp.sum(dqkv[halo:, 0:width].astype(F32), axis=0, keepdims=True)
+    vec[1:2] = jnp.sum(dqkv[:, 2 * width :].astype(F32), axis=0, keepdims=True)
+
+    for j in range(6):
+        for yy in range(2):
+            c0 = yy * (3 * width // 2) + j * 256
+            for m in range(width // 256):
+                put(2 + j, yy, m, dot(act1t[m * 256 : (m + 1) * 256], dqkv[:, c0 : c0 + 256]))
+        core_copy(10 + j).start()
+        if j % 2 == 1:
+            event(6 + j // 2)
+
+    def wload(j, slot):
+        return pltpu.make_async_copy(wqkv_hbm.at[:, pl.ds(j * 512, 512)], wbuf.at[slot], wsem.at[slot])
+
+    order = [2, 3, 4, 5, 0, 1]
+    wload(order[0], 0).start()
+    for i, j in enumerate(order):
+        wload(j, i % 2).wait()
+        if i + 1 < 6:
+            wload(order[i + 1], (i + 1) % 2).start()
+        cols = slice(j * 512, (j + 1) * 512)
+        if i < 4:
+            part = dot_nt(dqkv[0:halo, cols], wbuf[i % 2])
+            if i == 0:
+                dnh[...] = part
+            else:
+                dnh[...] += part
+        for m in range(tokens // 256):
+            part = dot_nt(dqkv[halo + m * 256 : halo + (m + 1) * 256, cols], wbuf[i % 2])
+            if i == 0:
+                dn1[m * 256 : (m + 1) * 256] = part
+            else:
+                dn1[m * 256 : (m + 1) * 256] += part
+        if i == 3:
+            dnc[0] = dnh[...].astype(BF16)
+
+    back = pltpu.make_async_remote_copy(
+        src_ref=dnc.at[0], dst_ref=dnc.at[1], send_sem=hs, recv_sem=hr, device_id=partner("y"), device_id_type=MESH,
+    )
+
+    @pl.when(seq == 1)
+    def _():
+        back.start()
+
+    event(9)
+
+    @pl.when(seq == 1)
+    def _():
+        back.wait_send()
+
+    @pl.when(seq == 0)
+    def _():
+        back.wait_recv()
+        dn1[tokens - halo :] += dnc[1].astype(F32)
+
+    gain1 = g1_ref[...].astype(F32)
+
+    def norm_rows(r, carry):
+        rows = pl.ds(pl.multiple_of(r * 64, 64), 64)
+        v = x_ref[rows].astype(F32)
+        center = v - jnp.mean(v, axis=-1, keepdims=True)
+        inv = lax.rsqrt(jnp.mean(center * center, axis=-1, keepdims=True) + norm_eps)
+        normed = center * inv
+        dn = dn1[rows]
+        e = dn * gain1
+        vec[3:4] += jnp.sum(dn * normed, axis=0, keepdims=True)
+        vec[4:5] += jnp.sum(dn, axis=0, keepdims=True)
+        gin[rows] = dx2[rows] + inv * (
+            e - jnp.mean(e, axis=-1, keepdims=True) - normed * jnp.mean(e * normed, axis=-1, keepdims=True)
+        )
+        return carry
+
+    lax.fori_loop(0, tokens // 64, norm_rows, 0)
+
+    def vec_copy(i, kind):
+        return pltpu.make_async_remote_copy(
+            src_ref=vin.at[i, 0], dst_ref=vin.at[i, 1], send_sem=vs.at[i], recv_sem=vr.at[i],
+            device_id=partner(kind), device_id_type=MESH,
+        )
+
+    vin[0, 0] = vec[...]
+    kinds = ("c", "x", "y", "a", "b")
+    for i, kind in enumerate(kinds):
+        vec_copy(i, kind).start()
+        event(10 + i)
+        vec_copy(i, kind).wait()
+        total = vin[i, 0] + vin[i, 1]
+        if i < 4:
+            vin[i + 1, 0] = total
+        else:
+            vec[...] = total
+    for t in range(15, CHUNKS + 4):
+        event(t)
+
+
+def vmem():
+    return pl.BlockSpec(memory_space=pltpu.VMEM)
+
+
+def hbm():
+    return pl.BlockSpec(memory_space=pl.ANY)
+
+
+def shape(dims, dtype):
+    return jax.ShapeDtypeStruct(dims, dtype)
+
+
+DMA = pltpu.SemaphoreType.DMA
+
+
+def params(cid):
+    return pltpu.CompilerParams(collective_id=cid, has_side_effects=True, vmem_limit_bytes=63 * 2**20)
+
+
+def fast_local(
+    inputs, doc_ids, w_qkv, bias_q, bias_v, w_out, bias_out, norm1_gain, norm1_bias, norm2_gain, norm2_bias,
+    w_up, bias_up, w_down, bias_down, cotangent,
+):
+    x = inputs[0]
+    tokens, width = x.shape
+    ff = w_up.shape[1]
+    halo = 256
+    ext = tokens + halo
+    heads = width // HEAD_DIM
+    row = lambda v: v.reshape(1, -1)
+    docs = jnp.broadcast_to(doc_ids, (8, tokens))
+    slopes = jnp.asarray(
+        np.broadcast_to((2.0 ** -(np.arange(heads) + 1.0) * LOG2E)[:, None], (heads, 128)).astype(np.float32)
+    )
+    act2, act2t, x2, qkv, ot, act1t, dist = pl.pallas_call(
+        functools.partial(kernel_one, halo),
+        out_shape=(
+            shape((tokens, width), BF16), shape((width, tokens), BF16), shape((tokens, width), F32),
+            shape((ext, 3 * width), BF16), shape((width, tokens), BF16), shape((width, ext), BF16),
+            shape((2, 512, 256), F32),
+        ),
+        in_specs=[vmem()] * 10 + [hbm()] * 2,
+        out_specs=(hbm(),) * 7,
+        scratch_shapes=[
+            pltpu.VMEM((ext, width), BF16), pltpu.VMEM((width, ext), BF16), pltpu.VMEM((ext, 3 * width), BF16),
+            pltpu.VMEM((tokens, width), BF16), pltpu.VMEM((width, tokens), BF16), pltpu.VMEM((tokens, width), BF16),
+            pltpu.VMEM((width, tokens), BF16), pltpu.VMEM((tokens, width), F32), pltpu.VMEM((2, 512, 256), F32),
+            pltpu.VMEM((halo, width), BF16), pltpu.VMEM((8, tokens), jnp.int32), pltpu.VMEM((1, 3 * width), F32),
+            pltpu.VMEM((width, 3 * width), BF16), pltpu.VMEM((width, width), BF16),
+            DMA((7,)), DMA((7,)), DMA((2,)), DMA((2,)),
+        ],
+        compiler_params=params(0),
+        name="attention_forward",
+    )(
+        x, docs, slopes, row(bias_q), row(bias_v), row(bias_out), row(norm1_gain), row(norm1_bias), row(norm2_gain),
+        row(norm2_bias), w_qkv, w_out,
+    )
+    cot = cotangent[0]
+    steps = ff // 512
+    out, g_w_up, dx2, ab, hd, vec = pl.pallas_call(
+        kernel_two,
+        out_shape=(
+            shape((tokens, width), BF16), shape((width // 16, ff // 2), F32), shape((tokens, width), F32),
+            shape((tokens, width), BF16), shape((8, 32, 32, 256), BF16), shape((16, width), F32),
+        ),
+        in_specs=[vmem()] * 7 + [hbm()] * 2,
+        out_specs=(vmem(), vmem(), vmem(), vmem(), hbm(), vmem()),
+        scratch_shapes=[
+            pltpu.VMEM((ff, tokens), BF16), pltpu.VMEM((tokens, 512), BF16), pltpu.VMEM((tokens, 512), BF16),
+            pltpu.VMEM((tokens, width), F32), pltpu.VMEM((tokens, width), F32),
+            pltpu.VMEM((2, width, 512), BF16), pltpu.VMEM((2, 512, width), BF16),
+            pltpu.VMEM((2, 2, 32, 32, 256), BF16), pltpu.VMEM((steps, 32, 32, 256), BF16),
+            pltpu.VMEM((steps, 32, 32, 256), BF16),
+        ]
+        + arrival_shapes(steps)
+        + [
+            pltpu.VMEM((2, 2, 4, 32, 32, 256), BF16), pltpu.VMEM((2, 4, 32, 32, 256), BF16),
+            DMA((2, 4)), DMA((2,)), DMA((steps,)), DMA((4, steps, 2)), DMA((4, steps, 2)), DMA((2,)), DMA((2,)),
+            DMA((2,)),
+        ],
+        compiler_params=params(1),
+        name="feed_forward",
+    )(act2, act2t, cot, x2, row(norm2_gain), row(bias_up), row(bias_down), w_up, w_down)
+
+    gin, g_w_down, g_w_out, g_w_qkv, vec = pl.pallas_call(
+        functools.partial(kernel_three, halo),
+        out_shape=(
+            shape((tokens, width), F32), shape((ff // 16, width // 2), F32), shape((width // 16, width // 2), F32),
+            shape((width // 16, 3 * width // 2), F32), shape((16, width), F32),
+        ),
+        in_specs=[vmem()] * 10 + [hbm()] * 3,
+        out_specs=(vmem(),) * 5,
+        scratch_shapes=[
+            pltpu.VMEM((tokens, width), BF16), pltpu.VMEM((ext, 3 * width), BF16), pltpu.VMEM((tokens, width), F32),
+            pltpu.VMEM((halo, width), F32), pltpu.VMEM((2, halo, width), BF16), pltpu.VMEM((2, width, 512), BF16),
+            pltpu.VMEM((width, width), BF16),
+            pltpu.VMEM((8, 2, 32, 32, 256), BF16), pltpu.VMEM((8, 32, 32, 256), BF16),
+            pltpu.VMEM((CHUNKS, 32, 32, 256), BF16),
+        ]
+        + arrival_shapes(CHUNKS)
+        + [
+            pltpu.VMEM((5, 2, 16, width), F32),
+            DMA((3,)), DMA((8,)), DMA((8,)), DMA((4, CHUNKS, 2)), DMA((4, CHUNKS, 2)), DMA((1,)), DMA, DMA,
+            DMA((5,)), DMA((5,)),
+        ],
+        compiler_params=params(2),
+        name="attention_backward",
+    )(x, slopes, row(norm1_gain), ab, dx2, qkv, ot, act1t, dist, vec, hd, w_qkv, w_out)
+    return (
+        out[None], gin[None], g_w_qkv, vec[0], vec[1], g_w_out, vec[2], vec[3], vec[4], vec[5], vec[6], g_w_up,
+        vec[8 : 8 + ff // width].reshape(ff), g_w_down, vec[7],
+    )
 
 
 def smooth_act(values):
@@ -361,4 +1137,6 @@
         P("dp", "seq"),
         P(),
     )
-    return jax.shard_map(local, mesh=mesh, in_specs=in_specs, out_specs=out_specs, check_vma=False)
+    sizes = (mesh.shape["dp"], mesh.shape["seq"])
+    chosen = fast_local if sizes == (16, 2) else local
+    return jax.shard_map(chosen, mesh=mesh, in_specs=in_specs, out_specs=out_specs, check_vma=False)

time: 845 us -> 236 us (0.28); the launches traced: 835 us -> 235 us
  waiting for transfers between devices: 325 us -> 0 us
  matrix products: 214 us -> 0 us
  Pallas kernels: 0 us -> 212 us
  local copies, waits for them, and re-layouts: 104 us -> 22.8 us
  other arithmetic: 56.2 us -> 0 us
  blocking collectives: 54.2 us -> 0 us
  starting transfers between devices: 33.6 us -> 0 us
  loops' own time: 33 us -> 0 us
  between operations: 15.4 us -> 0.69 us
    reduce_scatter x8 -> x0, waiting for transfers between devices: 263 us -> none  [the longest x1 98.8 us: local(): lax.psum_scatter(matrices[3].astype(jnp.bfloat16), 'dp', scatter_dimensio...]
    dot_general x68 -> x0, matrix products: 214 us -> none  [the longest x16 45.7 us: block_scores(): lax.dot_general(query_block, key_rows, (((1,), (1,)), ((), ())), preferre...]
    pallas_call x0 -> x3, Pallas kernels: none -> 212 us  [the longest x1 112 us: fast_local(): pl.pallas_call(functools.partial(kernel_three, halo), out_shape=(shape((t...]
    all_to_all x8 -> x0, waiting for transfers between devices: 61.7 us -> none  [the longest x1 12.7 us: local(): lax.all_to_all(query_rows, 'seq', split_axis=1, concat_axis=0, tiled=True)]
    psum x1 -> x0, blocking collectives: 41.7 us -> none  [local(): lax.psum((g_bias_q, g_bias_v, g_bias_out, g_gain_one, g_shift_one, g_gain...]
    another operation x10 -> x0, loops' own time: 33 us -> none  [the longest x4 17 us: head_backward(): lax.scan(one_block, (zeros_block, zeros_block), starts)]
    all_to_all x8 -> x0, starting transfers between devices: 32.8 us -> none  [the longest x1 4.95 us: local(): lax.all_to_all(jnp.moveaxis(head_outs, 0, 1), 'seq', split_axis=0, concat...]
    squeeze x24 -> x0, local copies, waits for them, and re-layouts: 23.8 us -> none  [local(): lax.map(forward_head, (head_q, head_k, head_v, slopes))]
  transfers between devices with their start and end apart: 16 -> 0, of which waited for: 11 -> 0; matrix products, arithmetic and copies ran while one was open for 24% -> 0% of each run, Pallas kernels for 0% -> 0%
where the time goes in v1:
time: 236 us; the launch traced here: 235 us
  Pallas kernels  212 us (90%)
  local copies, waits for them, and re-layouts  22.8 us (10%)
    pallas_call x1, Pallas kernels, fast_local(): pl.pallas_call(functools.partial(kernel_three, halo), out_shape=(shape((t...  112 us
    pallas_call x1, Pallas kernels, fast_local(): pl.pallas_call(kernel_two, out_shape=(shape((tokens, width), BF16), shape...  71.7 us
    pallas_call x1, Pallas kernels, fast_local(): pl.pallas_call(functools.partial(kernel_one, halo), out_shape=(shape((tok...  28 us
    reshape x9, local copies, waits for them, and re-layouts, fast_local(): row = lambda v: v.reshape(1, -1)  11.5 us
    unnamed x18, local copies, waits for them, and re-layouts  8.11 us

profile of v1, /device:TPU:0, one launch (start us, length us, event | category | flops | bytes accessed | tf_op | source)
XLA Modules:
  0.0 235.2 jit_solution(17622760604985122356)
XLA Ops:
  0.6 1.3 reshape.65.g1_ref
  1.9 1.3 reshape.67.g2_ref
  3.2 1.3 reshape.62.bq_ref
  4.5 1.3 reshape.63.bv_ref
  5.8 1.3 reshape.64.bo_ref
  7.0 1.3 reshape.66.s1_ref
  8.3 1.3 reshape.68.s2_ref
  9.6 1.3 reshape.70.bdown_ref
  10.9 1.3 broadcast_in_dim.14.doc_ref
  12.2 1.3 reshape.69.bup_ref
  13.5 28.0 %attention_forward.1 = (bf16[512,1024]{1,0:T(8,128)(2,1)}, bf16[1024,512]{1,0:T(8,128)(2,1)}, f32[512,1024]{1,0:T(8,128)}, bf16[768,3072]{1,0:T(8,128)(2,1)}, bf...) custom-call(bf16[512,1024]{1,0:T(8,128)(2,1)} %bitcast.18, ...), custom_call_target="tpu_custom_call" | custom-call | tf_op jit(solution)/shard_map/attention_forward/pallas_call | solution.py:709
  41.5 71.7 %feed_forward.1 = (bf16[512,1024]{1,0:T(8,128)(2,1)}, f32[64,2048]{1,0:T(8,128)}, f32[512,1024]{1,0:T(8,128)}, bf16[512,1024]{1,0:T(8,128)(2,1)}, bf16[8,32,32,256]{3,2,1,0:T(8,128)(2,1)}, /*index=5*/f32[16,1024]{1,0:T(8,128)}) custom-call(bf16[512,1024]{1,0:T(8,128)(2,1)} %get-tuple-element.33.act2, bf16[1024,512]{1,0:T(8,128)(2,1)} %get-tuple-element.34.act2t, ...), custom_call_target="tpu_custom_call" | custom-call | tf_op jit(solution)/shard_map/feed_forward/pallas_call | solution.py:734
  113.2 112.0 %attention_backward.1 = (f32[512,1024]{1,0:T(8,128)}, f32[256,512]{1,0:T(8,128)}, f32[64,512]{1,0:T(8,128)}, f32[64,1536]{1,0:T(8,128)}, f32[16,1024]{1,0:T(8,128)}) custom-call(bf16[512,1024]{1,0:T(8,128)(2,1)} %bitcast.19, f32[8,128]{1,0:T(8,128)} %constant.2.clone.slope_ref, bf16[1,1024]{1,0:T(2,128)(2,1)} %reshape.65.g1_ref, ...), custom_call_target="tpu_custom_call" | custom-call | tf_op jit(solution)/shard_map/attention_backward/pallas_call | solution.py:759
  225.2 0.0 copy-start
  225.2 0.9 slice_bitcast_fusion
  226.1 1.9 fusion
  228.0 0.6 copy.34
  228.6 2.3 copy.41
  230.8 0.0 copy-done
  230.8 0.0 copy-start.3
  230.8 0.0 copy-start.4
  230.8 0.0 copy-start.1
  230.8 1.3 copy.42
  232.2 0.0 copy-done.3
  232.2 0.0 copy-start.2
  232.2 0.7 copy.43
  232.9 0.0 copy-done.4
  232.9 0.7 copy.44
  233.6 0.0 copy-done.1
  233.6 0.8 copy.45
  234.4 0.0 copy-done.2
  234.4 0.8 copy.46
Async XLA Ops:
  225.2 5.7 %copy-start = (f32[512,1024]{1,0:T(8,128)S(1)}, f32[512,1024]{1,0:T(8,128)}, u32[]{:S(2)}) copy-start(f32[512,1024]{1,0:T(8,128)} %get-tuple-element.45) | copy-start | bytes 6291460
  230.8 1.3 copy-start.3
  230.8 2.1 copy-start.4
  230.8 2.7 %copy-start.1 = (f32[64,2048]{1,0:T(8,128)S(1)}, f32[64,2048]{1,0:T(8,128)}, u32[]{:S(2)}) copy-start(f32[64,2048]{1,0:T(8,128)} %get-tuple-element.85) | copy-start | bytes 1572868
  232.2 2.2 copy-start.2

commit v2 on v0

--- a/solution.py
+++ b/solution.py
@@ -1,13 +1,792 @@
+import functools
+
 import jax
 import jax.numpy as jnp
+import numpy as np
 from jax import lax
+from jax.experimental import pallas as pl
+from jax.experimental.pallas import tpu as pltpu
 from jax.sharding import PartitionSpec as P
 
 HEAD_DIM = 128
-
+MESH = pl.DeviceIdType.MESH
+F32 = jnp.float32
+BF16 = jnp.bfloat16
+LOG2E = 1.4426950408889634
+FAR = 1e30
+GELU_C = 0.7978845608028654
+GELU_A = 0.044715
 
 norm_eps = 1e-05
 masked_score = -1e30
+
+NT = (((1,), (1,)), ((), ()))
+TN = (((0,), (0,)), ((), ()))
+
+
+def dot(a, b):
+    return jnp.dot(a, b, preferred_element_type=F32)
+
+
+def dot_nt(a, b):
+    return lax.dot_general(a, b, NT, preferred_element_type=F32)
+
+
+def dot_tn(a, b):
+    return lax.dot_general(a, b, TN, preferred_element_type=F32)
+
+
+def coords():
+    dp = lax.axis_index("dp")
+    return {
+        "c": dp % 2,
+        "x": (dp // 2) % 2,
+        "a": (dp // 4) % 2,
+        "b": dp // 8,
+        "y": lax.axis_index("seq"),
+    }
+
+
+def partner(kind):
+    dp = lax.axis_index("dp")
+    if kind == "y":
+        return {"seq": 1 - lax.axis_index("seq")}
+    step = {"c": 1, "x": 2, "a": 4, "b": 8}[kind]
+    bit = (dp // step) % 2
+    return {"dp": dp + step - 2 * step * bit}
+
+
+def greet(kinds):
+    barrier = pltpu.get_barrier_semaphore()
+    for kind in kinds:
+        pl.semaphore_signal(barrier, inc=1, device_id=partner(kind), device_id_type=MESH)
+    pl.semaphore_wait(barrier, len(kinds))
+
+
+ORDERS = (("x", "a", "y", "b"), ("y", "a", "x", "b"))
+
+
+def block_index(half, place):
+    index = half * 16
+    for kind, weight in zip(ORDERS[half], (8, 4, 2, 1)):
+        index = index + place[kind] * weight
+    return index
+
+
+def dp_bits(dp):
+    return {"c": dp % 2, "x": (dp // 2) % 2, "a": (dp // 4) % 2, "b": dp // 8}
+
+
+class Scatter:
+    def __init__(self, held, arrivals, send_sem, recv_sem):
+        self.held, self.arrivals = held, arrivals
+        self.send_sem, self.recv_sem = send_sem, recv_sem
+        self.me = coords()
+
+    def offset(self, half, stage, other):
+        index = half * 16
+        for k, weight in zip(range(stage + 1), (8, 4, 2, 1)):
+            bit = self.me[ORDERS[half][k]]
+            if other and k == stage:
+                bit = 1 - bit
+            index = index + bit * weight
+        return index
+
+    def copy(self, chunk, stage, half):
+        size = 8 >> stage
+        return pltpu.make_async_remote_copy(
+            src_ref=self.held.at[chunk, pl.ds(self.offset(half, stage, True), size)],
+            dst_ref=self.arrivals[stage].at[chunk, half],
+            send_sem=self.send_sem.at[stage, chunk, half],
+            recv_sem=self.recv_sem.at[stage, chunk, half],
+            device_id=partner(ORDERS[half][stage]),
+            device_id_type=MESH,
+        )
+
+    def start(self, chunk, stage):
+        for half in range(2):
+            self.copy(chunk, stage, half).start()
+
+    def finish(self, chunk, stage):
+        size = 8 >> stage
+        for half in range(2):
+            self.copy(chunk, stage, half).wait()
+            mine = pl.ds(self.offset(half, stage, False), size)
+            self.held[chunk, mine] = self.held[chunk, mine] + self.arrivals[stage][chunk, half]
+
+    def result(self, chunk, half):
+        return self.held[chunk, self.offset(half, 3, False)]
+
+
+def arrival_shapes(chunks):
+    return [pltpu.VMEM((chunks, 2, 8 >> k, 32, 256), BF16) for k in range(4)]
+
+
+def when(cond, fn):
+    if isinstance(cond, (bool, np.bool_)):
+        if cond:
+            fn()
+    else:
+        pl.when(cond)(fn)
+
+
+def inside(value, low, high):
+    if isinstance(value, int):
+        return low <= value < high
+    return (value >= low) & (value < high)
+
+
+RING = 3
+AHEAD = 3
+
+
+def row_of(ref):
+    return ref[...].astype(F32).reshape(1, -1)
+
+
+def layer_kernel(
+    halo, x_ref, doc_ref, slope_ref, bq_ref, bv_ref, bo_ref, g1_ref, s1_ref, g2_ref, s2_ref, bup_ref, bdown_ref,
+    cot_hbm, wqkv_hbm, wout_hbm, wup_hbm, wdown_hbm,
+    out_hbm, gin_hbm, gup, gdown, gout, gqkv, vec,
+    qkv, act1t, ot, dist, doch, x2, cot, act2, act2t, hid_t, dpre, dn2, dn1, dnh, dqkv, wu, wd, bias, bup,
+    grad, held, r1, r2, r3, r4, vin,
+    qsem, osem, wsem, csem, cs, cr, ss, rs, hs, hr, vs, vr, esem,
+):
+    tokens, width = x_ref.shape
+    heads = width // HEAD_DIM
+    ff = wup_hbm.shape[1]
+    half_ff = ff // 2
+    steps = half_ff // 256
+    seq = lax.axis_index("seq")
+    me = coords()
+    first_down, first_out, first_qkv, chunks = steps, 2 * steps, 2 * steps + 2, 2 * steps + 8
+    scale = HEAD_DIM**-0.5
+
+    act1 = dqkv.at[:, pl.ds(0, width)]
+    o_s = dqkv.at[pl.ds(halo, tokens), pl.ds(width, width)]
+    xh = dqkv.at[pl.ds(0, halo), pl.ds(2 * width, width)]
+    wout_low = dqkv.at[pl.ds(halo, 512), pl.ds(2 * width, width)]
+
+    dn_come = qkv.at[pl.ds(0, halo), pl.ds(0, width)]
+    dn_send = qkv.at[pl.ds(0, halo), pl.ds(width, width)]
+
+    def wqkv_part(j):
+        return wu.at[j] if j < 2 else hid_t.at[pl.ds((j - 2) * width, width)]
+
+    qloads = [
+        pltpu.make_async_copy(wqkv_hbm.at[:, pl.ds(j * 512, 512)], wqkv_part(j), qsem.at[j]) for j in range(6)
+    ]
+    oloads = [
+        pltpu.make_async_copy(wout_hbm.at[pl.ds(0, 512)], wout_low, osem.at[0]),
+        pltpu.make_async_copy(wout_hbm.at[pl.ds(512, 512)], wd.at[1], osem.at[1]),
+    ]
+    cload = pltpu.make_async_copy(cot_hbm, cot, csem)
+    for cp in qloads + oloads + [cload]:
+        cp.start()
+    greet(("c", "x", "a", "b", "y"))
+    send_x = pltpu.make_async_remote_copy(
+        src_ref=x_ref.at[pl.ds(tokens - halo, halo)], dst_ref=xh, send_sem=hs.at[0], recv_sem=hr.at[0],
+        device_id=partner("y"), device_id_type=MESH,
+    )
+    send_doc = pltpu.make_async_remote_copy(
+        src_ref=doc_ref, dst_ref=doch, send_sem=hs.at[1], recv_sem=hr.at[1],
+        device_id=partner("y"), device_id_type=MESH,
+    )
+
+    @pl.when(seq == 0)
+    def _():
+        send_doc.start()
+        send_x.start()
+
+    def weights(f, slot):
+        col = pl.multiple_of(f * 256, 256)
+        return [
+            pltpu.make_async_copy(wup_hbm.at[:, pl.ds(col, 256)], wu.at[slot, :, pl.ds(0, 256)], wsem.at[slot, 0]),
+            pltpu.make_async_copy(
+                wup_hbm.at[:, pl.ds(half_ff + col, 256)], wu.at[slot, :, pl.ds(256, 256)], wsem.at[slot, 1]
+            ),
+            pltpu.make_async_copy(wdown_hbm.at[pl.ds(col, 256)], wd.at[slot, pl.ds(0, 256)], wsem.at[slot, 2]),
+            pltpu.make_async_copy(
+                wdown_hbm.at[pl.ds(half_ff + col, 256)], wd.at[slot, pl.ds(256, 256)], wsem.at[slot, 3]
+            ),
+        ]
+
+    scatter = Scatter(held, (r1, r2, r3, r4), ss, rs)
+
+    def core_copy(n):
+        return pltpu.make_async_remote_copy(
+            src_ref=grad.at[n % RING, 1 - me["c"]], dst_ref=held.at[n], send_sem=cs.at[n % RING], recv_sem=cr.at[n],
+            device_id=partner("c"), device_id_type=MESH,
+        )
+
+    def join(n):
+        core_copy(n).wait()
+        held[n] = held[n] + grad[n % RING, me["c"]]
+
+    def put(n, yy, m, tile):
+        for q in range(4):
+            place = dp_bits(m * 4 + q)
+            place["y"] = yy
+            for h in range(2):
+                r0 = q * 64 + h * 32
+                grad[n % RING, place["c"], block_index(h, place)] = tile[r0 : r0 + 32].astype(BF16)
+
+    def store(n):
+        for h in range(2):
+            block = scatter.result(n, h)
+
+            def up():
+                gup[h * 32 : h * 32 + 32, pl.ds(pl.multiple_of(n * 256, 256), 256)] = block
+
+            def down():
+                i = n - first_down
+                row = pl.multiple_of((i % 4) * 64 + h * 32, 32)
+                gdown[pl.ds(row, 32), pl.ds(pl.multiple_of((i // 4) * 256, 256), 256)] = block
+
+            def outp():
+                gout[h * 32 : h * 32 + 32, pl.ds(pl.multiple_of((n - first_out) * 256, 256), 256)] = block
+
+            def proj():
+                gqkv[h * 32 : h * 32 + 32, pl.ds(pl.multiple_of((n - first_qkv) * 256, 256), 256)] = block
+
+            when(inside(n, 0, first_down), up)
+            when(inside(n, first_down, first_out), down)
+            when(inside(n, first_out, first_qkv), outp)
+            when(inside(n, first_qkv, chunks), proj)
+
+    def service(t, ahead=True):
+        if ahead:
+            when(inside(t + AHEAD, 0, chunks), lambda: scatter.start(t + AHEAD, 0))
+
+        def last():
+            scatter.finish(t - 6, 3)
+            store(t - 6)
+
+        when(inside(t - 6, 0, chunks), last)
+        for stage in (2, 1, 0):
+            n = t - 2 * stage
+
+            def step(stage=stage, n=n):
+                scatter.finish(n, stage)
+                scatter.start(n, stage + 1)
+
+            when(inside(n, 0, chunks), step)
+
+    gain1, shift1 = row_of(g1_ref), row_of(s1_ref)
+    gain2, shift2 = row_of(g2_ref), row_of(s2_ref)
+
+    def norm(v, gain, shift):
+        center = v - jnp.mean(v, axis=-1, keepdims=True)
+        inv = lax.rsqrt(jnp.mean(center * center, axis=-1, keepdims=True) + norm_eps)
+        return center * inv * gain + shift
+
+    bias[:, 0:width] = row_of(bq_ref)
+    bias[:, width : 2 * width] = jnp.zeros((1, width), F32)
+    bias[:, 2 * width :] = row_of(bv_ref)
+    bup[...] = row_of(bup_ref)
+
+    for r in range(tokens // 128):
+        v = norm(x_ref[r * 128 : (r + 1) * 128].astype(F32), gain1, shift1).astype(BF16)
+        act1[halo + r * 128 : halo + (r + 1) * 128] = v
+        act1t[:, halo + r * 128 : halo + (r + 1) * 128] = v.T
+
+    for j in range(6):
+        qloads[j].wait()
+        cols = slice(j * 512, (j + 1) * 512)
+        for m in range(tokens // 256):
+            rows = slice(halo + m * 256, halo + (m + 1) * 256)
+            qkv[rows, cols] = (dot(act1[rows], wqkv_part(j)[...]) + bias[:, cols]).astype(BF16)
+    for cp in weights(0, 0):
+        cp.start()
+
+    own_doc = doc_ref[...].astype(F32)
+    own_cols = jnp.transpose(jnp.broadcast_to(own_doc, (128, tokens)))[:, 0:1]
+
+    def distances(block, key_docs):
+        keys = key_docs[block * 256 : block * 256 + 512]
+        queries = own_doc[:, block * 256 : block * 256 + 256]
+        key_pos = lax.broadcasted_iota(jnp.int32, (512, 256), 0)
+        query_pos = lax.broadcasted_iota(jnp.int32, (512, 256), 1) + 256
+        gap = query_pos - key_pos
+        allowed = (gap >= 0) & (keys == queries)
+        dist[block] = jnp.where(allowed, gap.astype(F32), FAR)
+
+    def attend(block):
+        def some_heads(i, carry):
+            for u in range(FWD_HEADS):
+                h = i * FWD_HEADS + u
+                c0 = pl.multiple_of(h * HEAD_DIM, HEAD_DIM)
+                q = qkv[halo + block * 256 : halo + (block + 1) * 256, pl.ds(c0, HEAD_DIM)]
+                k = qkv[block * 256 : block * 256 + 512, pl.ds(width + c0, HEAD_DIM)]
+                v = qkv[block * 256 : block * 256 + 512, pl.ds(2 * width + c0, HEAD_DIM)]
+                slope = slope_ref[pl.ds(h, 1), 0:1]
+                s = dot_nt(k, q) * (LOG2E * scale) - slope * dist[block]
+                e = jnp.exp2(s - jnp.max(s, axis=0, keepdims=True))
+                p = (e * (1.0 / jnp.sum(e, axis=0, keepdims=True))).astype(BF16)
+                o_t = dot_tn(v, p)
+                ot[pl.ds(c0, HEAD_DIM), block * 256 : (block + 1) * 256] = o_t.astype(BF16)
+                o_s[block * 256 : (block + 1) * 256, pl.ds(c0, HEAD_DIM)] = o_t.T.astype(BF16)
+            return carry
+
+        lax.fori_loop(0, heads // FWD_HEADS, some_heads, 0)
+
+    def project(block):
+        for r in range(2):
+            rows = slice(block * 256 + r * 128, block * 256 + (r + 1) * 128)
+            second = (
+                x_ref[rows].astype(F32) + dot(o_s[rows, 0:512], wout_low[...]) + dot(o_s[rows, 512:1024], wd[1])
+            ) + row_of(bo_ref)
+            x2[rows] = second
+            v = norm(second, gain2, shift2).astype(BF16)
+            act2[rows] = v
+            act2t[:, rows] = v.T
+
+    distances(1, jnp.concatenate([jnp.full((halo, 1), -1.0, F32), own_cols], axis=0))
+    attend(1)
+    for cp in oloads:
+        cp.wait()
+    project(1)
+
+    @pl.when(seq == 0)
+    def _():
+        send_doc.wait_send()
+        send_x.wait_send()
+        doch[...] = jnp.full(doch.shape, -1, jnp.int32)
+        act1t[:, 0:halo] = jnp.zeros((width, halo), BF16)
+        qkv[0:halo, width:] = jnp.zeros((halo, 2 * width), BF16)
+
+    @pl.when(seq == 1)
+    def _():
+        send_doc.wait_recv()
+        send_x.wait_recv()
+        for r in range(halo // 128):
+            v = norm(xh[r * 128 : (r + 1) * 128].astype(F32), gain1, shift1).astype(BF16)
+            act1[r * 128 : (r + 1) * 128] = v
+            act1t[:, r * 128 : (r + 1) * 128] = v.T
+        for j in range(2, 6):
+            cols = slice(j * 512, (j + 1) * 512)
+            qkv[0:halo, cols] = (dot(act1[0:halo], wqkv_part(j)[...]) + bias[:, cols]).astype(BF16)
+
+    halo_doc = doch[...].astype(F32)[:, tokens - halo :]
+    halo_cols = jnp.transpose(jnp.broadcast_to(halo_doc, (128, halo)))[:, 0:1]
+    distances(0, jnp.concatenate([halo_cols, own_cols], axis=0))
+    attend(0)
+    project(0)
+
+    cload.wait()
+    vec[...] = jnp.zeros(vec.shape, F32)
+    vec[7:8] = jnp.sum(cot[...].astype(F32), axis=0, keepdims=True)
+    dn2[...] = jnp.zeros(dn2.shape, F32)
+
+    def ff_step(f, carry):
+        slot = f % 2
+        for cp in weights(f, slot):
+            cp.wait()
+
+        @pl.when(f + 1 < steps)
+        def _():
+            for cp in weights(f + 1, 1 - slot):
+                cp.start()
+
+        for yy in range(2):
+            cols = slice(yy * 256, (yy + 1) * 256)
+            first = pl.multiple_of(yy * half_ff + f * 256, 256)
+            shift = bup[:, pl.ds(first, 256)]
+            sums = jnp.zeros((1, 256), F32)
+            for m in range(tokens // 256):
+                rows = slice(m * 256, (m + 1) * 256)
+                u = dot(act2[rows], wu[slot, :, cols]) + shift
+                dh = dot_nt(cot[rows], wd[slot, cols])
+                uu = u * u
+                th = jnp.tanh(GELU_C * u * (1.0 + GELU_A * uu))
+                half_u = 0.5 * u
+                hv = (half_u * (1.0 + th)).astype(BF16)
+                slope = 0.5 * (1.0 + th) + half_u * (1.0 - th * th) * (GELU_C * (1.0 + 3.0 * GELU_A * uu))
+                dv = (dh * slope).astype(BF16)
+                dpre[rows, cols] = dv
+                hid_t[pl.ds(first, 256), rows] = hv.T
+                sums = sums + jnp.sum(dv.astype(F32), axis=0, keepdims=True)
+            row = yy * (half_ff // width) + f // (width // 256)
+            vec[pl.ds(8 + row, 1), pl.ds(pl.multiple_of((f % (width // 256)) * 256, 256), 256)] = sums
+
+        @pl.when(f >= 1)
+        def _():
+            join(f - 1)
+            scatter.start(f - 1, 0)
+
+        for yy in range(2):
+            cols = slice(yy * 256, (yy + 1) * 256)
+            for m in range(width // 256):
+                put(f, yy, m, dot(act2t[m * 256 : (m + 1) * 256], dpre[:, cols]))
+        core_copy(f).start()
+        for m in range(tokens // 256):
+            rows = slice(m * 256, (m + 1) * 256)
+            dn2[rows] += dot_nt(dpre[rows], wu[slot])
+        service(f - 3, ahead=False)
+        return carry
+
+    lax.fori_loop(0, steps, ff_step, 0)
+    join(steps - 1)
+    scatter.start(steps - 1, 0)
+    oloads = [pltpu.make_async_copy(wout_hbm.at[pl.ds(i * 512, 512)], wd.at[i], osem.at[i]) for i in range(2)]
+    order = (2, 3, 4, 5, 0, 1)
+
+    def qload(i):
+        return pltpu.make_async_copy(wqkv_hbm.at[:, pl.ds(order[i] * 512, 512)], wu.at[i % 2], qsem.at[i % 2])
+
+    for cp in oloads + [qload(0), qload(1)]:
+        cp.start()
+
+    def down_step(i, carry):
+        n = first_down + i
+        for yy in range(2):
+            right = cot[:, pl.ds(pl.multiple_of(yy * 512 + (i // 4) * 256, 256), 256)]
+            for m in range(4):
+                left = jnp.concatenate(
+                    [
+                        hid_t[pl.ds(pl.multiple_of((m * 4 + q) * 256 + (i % 4) * 64, 64), 64)]
+                        for q in range(4)
+                    ],
+                    axis=0,
+                )
+                put(n, yy, m, dot(left, right))
+        core_copy(n).start()
+
+        @pl.when(i >= 1)
+        def _():
+            join(n - 1)
+
+        for at, t in ((2, steps - 3), (5, steps - 2), (7, steps - 1)):
+
+            @pl.when(i == at)
+            def _(t=t):
+                service(t)
+
+        return carry
+
+    lax.fori_loop(0, steps, down_step, 0)
+    join(first_out - 1)
+
+    def norm_two(r, carry):
+        rows = pl.ds(pl.multiple_of(r * 64, 64), 64)
+        v = x2[rows]
+        center = v - jnp.mean(v, axis=-1, keepdims=True)
+        inv = lax.rsqrt(jnp.mean(center * center, axis=-1, keepdims=True) + norm_eps)
+        normed = center * inv
+        dn = dn2[rows]
+        e = dn * gain2
+        vec[5:6] += jnp.sum(dn * normed, axis=0, keepdims=True)
+        vec[6:7] += jnp.sum(dn, axis=0, keepdims=True)
+        dx = cot[rows].astype(F32) + inv * (
+            e - jnp.mean(e, axis=-1, keepdims=True) - normed * jnp.mean(e * normed, axis=-1, keepdims=True)
+        )
+        dn2[rows] = dx
+        low = dx.astype(BF16)
+        cot[rows] = low
+        vec[2:3] += jnp.sum(low.astype(F32), axis=0, keepdims=True)
+        return carry
+
+    lax.fori_loop(0, tokens // 64, norm_two, 0)
+    dx2, ab, do = dn2, cot, act2
+    service(steps)
+
+    for j in range(2):
+        for yy in range(2):
+            c0 = yy * 512 + j * 256
+            for m in range(width // 256):
+                put(first_out + j, yy, m, dot(ot[m * 256 : (m + 1) * 256], ab[:, c0 : c0 + 256]))
+        core_copy(first_out + j).start()
+    service(steps + 1)
+    for cp in oloads:
+        cp.wait()
+    for m in range(tokens // 256):
+        rows = slice(m * 256, (m + 1) * 256)
+        for i in range(2):
+            do[rows, i * 512 : (i + 1) * 512] = dot_nt(ab[rows], wd[i]).astype(BF16)
+
+    def dload(i):
+        return pltpu.make_async_copy(wdown_hbm.at[pl.ds(i * 512, 512)], wd.at[i % 2], osem.at[i % 2])
+
+    dload(0).start()
+    dload(1).start()
+    join(first_out)
+    join(first_out + 1)
+    service(steps + 2)
+
+    dqkv[0:halo, 0:width] = jnp.zeros((halo, width), BF16)
+
+    def head_back(h):
+        c0 = pl.multiple_of(h * HEAD_DIM, HEAD_DIM)
+        slope = slope_ref[pl.ds(h, 1), 0:1]
+        parts = []
+        for block in range(2):
+            rows = slice(halo + block * 256, halo + (block + 1) * 256)
+            krows = slice(block * 256, block * 256 + 512)
+            q = qkv[rows, pl.ds(c0, HEAD_DIM)]
+            k = qkv[krows, pl.ds(width + c0, HEAD_DIM)]
+            v = qkv[krows, pl.ds(2 * width + c0, HEAD_DIM)]
+            g = do[block * 256 : (block + 1) * 256, pl.ds(c0, HEAD_DIM)]
+            s = dot_nt(k, q) * (LOG2E * scale) - slope * dist[block]
+            e = jnp.exp2(s - jnp.max(s, axis=0, keepdims=True))
+            p = e * (1.0 / jnp.sum(e, axis=0, keepdims=True))
+            dp = dot_nt(v, g)
+            delta = jnp.sum(p * dp, axis=0, keepdims=True)
+            ds = (p * (dp - delta)).astype(BF16)
+            dqkv[rows, pl.ds(c0, HEAD_DIM)] = (dot_tn(ds, k) * scale).astype(BF16)
+            parts.append((dot(ds, q) * scale, dot(p.astype(BF16), g)))
+        for which in range(2):
+            cols = pl.ds((1 + which) * width + c0, HEAD_DIM)
+            first, second = parts[0][which], parts[1][which]
+            dqkv[0:256, cols] = first[0:256].astype(BF16)
+            dqkv[256:512, cols] = (first[256:512] + second[0:256]).astype(BF16)
+            dqkv[512:768, cols] = second[256:512].astype(BF16)
+
+    def heads_back(i, carry):
+        for u in range(2):
+            head_back(i * 2 + u)
+        service(steps + 3 + i)
+        return carry
+
+    lax.fori_loop(0, heads // 2, heads_back, 0)
+    vec[0:1] = jnp.sum(dqkv[halo:, 0:width].astype(F32), axis=0, keepdims=True)
+    vec[1:2] = jnp.sum(dqkv[:, 2 * width :].astype(F32), axis=0, keepdims=True)
+
+    t0 = steps + 3 + heads // 2
+    for j in range(6):
+        n = first_qkv + j
+        for yy in range(2):
+            c0 = yy * (3 * width // 2) + j * 256
+            for m in range(width // 256):
+                put(n, yy, m, dot(act1t[m * 256 : (m + 1) * 256], dqkv[:, c0 : c0 + 256]))
+        core_copy(n).start()
+        if j >= 1:
+            join(n - 1)
+        if j % 2 == 1:
+            service(t0)
+            t0 += 1
+    join(chunks - 1)
+
+    for i, j in enumerate(order):
+        qload(i).wait()
+        cols = slice(j * 512, (j + 1) * 512)
+        if i < 4:
+            part = dot_nt(dqkv[0:halo, cols], wu[i % 2])
+            if i == 0:
+                dnh[...] = part
+            else:
+                dnh[...] += part
+        for m in range(tokens // 256):
+            part = dot_nt(dqkv[halo + m * 256 : halo + (m + 1) * 256, cols], wu[i % 2])
+            if i == 0:
+                dn1[m * 256 : (m + 1) * 256] = part
+            else:
+                dn1[m * 256 : (m + 1) * 256] += part
+        if i + 2 < 6:
+            qload(i + 2).start()
+        if i == 3:
+            dn_send[...] = dnh[...].astype(BF16)
+            back = pltpu.make_async_remote_copy(
+                src_ref=dn_send, dst_ref=dn_come, send_sem=hs.at[2], recv_sem=hr.at[2],
+                device_id=partner("y"), device_id_type=MESH,
+            )
+
+            @pl.when(seq == 1)
+            def _():
+                back.start()
+
+        if i % 2 == 1:
+            service(t0)
+            t0 += 1
+
+    def out_part(i):
+        dload(i).wait()
+        for m in range(tokens // 256):
+            rows = slice(m * 256, (m + 1) * 256)
+            part = dot_tn(hid_t[i * 512 : (i + 1) * 512, rows], wd[i % 2])
+            if i == 0:
+                part = part + row_of(bdown_ref)
+            if i < 7:
+                x2[rows] += part
+            else:
+                act2[rows] = (x2[rows] + part).astype(BF16)
+        if i + 2 < 8:
+            dload(i + 2).start()
+
+    for i in range(4):
+        out_part(i)
+    service(t0)
+    t0 += 1
+
+    @pl.when(seq == 1)
+    def _():
+        back.wait_send()
+
+    @pl.when(seq == 0)
+    def _():
+        back.wait_recv()
+        dn1[tokens - halo :] += dn_come[...].astype(F32)
+
+    def norm_one(r, carry):
+        rows = pl.ds(pl.multiple_of(r * 64, 64), 64)
+        v = x_ref[rows].astype(F32)
+        center = v - jnp.mean(v, axis=-1, keepdims=True)
+        inv = lax.rsqrt(jnp.mean(center * center, axis=-1, keepdims=True) + norm_eps)
+        normed = center * inv
+        dn = dn1[rows]
+        e = dn * gain1
+        vec[3:4] += jnp.sum(dn * normed, axis=0, keepdims=True)
+        vec[4:5] += jnp.sum(dn, axis=0, keepdims=True)
+        dn1[rows] = dx2[rows] + inv * (
+            e - jnp.mean(e, axis=-1, keepdims=True) - normed * jnp.mean(e * normed, axis=-1, keepdims=True)
+        )
+        return carry
+
+    lax.fori_loop(0, tokens // 64, norm_one, 0)
+    save_gin = pltpu.make_async_copy(dn1, gin_hbm, esem.at[0])
+    save_gin.start()
+
+    kinds = ("c", "x", "y", "a", "b")
+
+    def vec_copy(i):
+        return pltpu.make_async_remote_copy(
+            src_ref=vin.at[i, 0], dst_ref=vin.at[i, 1], send_sem=vs.at[i], recv_sem=vr.at[i],
+            device_id=partner(kinds[i]), device_id_type=MESH,
+        )
+
+    vin[0, 0] = vec[...]
+    vec_copy(0).start()
+    for i in range(5):
+        if i < 4:
+            out_part(4 + i)
+        if t0 < chunks:
+            service(t0)
+            t0 += 1
+        vec_copy(i).wait()
+        total = vin[i, 0] + vin[i, 1]
+        if i < 4:
+            vin[i + 1, 0] = total
+            vec_copy(i + 1).start()
+        else:
+            vec[...] = total
+        if i == 3:
+            save_out = pltpu.make_async_copy(act2, out_hbm, esem.at[1])
+            save_out.start()
+    for t in range(t0, chunks + 6):
+        service(t)
+    save_gin.wait()
+    save_out.wait()
+
+
+def finish_kernel(out_in, gin_in, gup, gdown, gout, gqkv, vec, *refs):
+    out, gin, o_qkv, bq, bv, o_out, bo, g1, s1, g2, s2, o_up, b_up, o_down, b_down = refs
+    out[...] = out_in[...]
+    gin[...] = gin_in[...]
+    o_qkv[...] = gqkv[...].astype(F32)
+    o_out[...] = gout[...].astype(F32)
+    o_up[...] = gup[...].astype(F32)
+    o_down[...] = gdown[...].astype(F32)
+    width = vec.shape[1]
+    for i, ref in enumerate((bq, bv, bo, g1, s1, g2, s2, b_down)):
+        ref[...] = vec[i]
+    for i in range(b_up.shape[0] // width):
+        b_up[i * width : (i + 1) * width] = vec[8 + i]
+
+
+FWD_HEADS = 2
+
+
+def vmem():
+    return pl.BlockSpec(memory_space=pltpu.VMEM)
+
+
+def hbm():
+    return pl.BlockSpec(memory_space=pl.ANY)
+
+
+def shape(dims, dtype):
+    return jax.ShapeDtypeStruct(dims, dtype)
+
+
+DMA = pltpu.SemaphoreType.DMA
+
+
+def params(cid):
+    return pltpu.CompilerParams(collective_id=cid, has_side_effects=True, vmem_limit_bytes=64 * 2**20 - 2**16)
+
+
+def fast_local(
+    inputs, doc_ids, w_qkv, bias_q, bias_v, w_out, bias_out, norm1_gain, norm1_bias, norm2_gain, norm2_bias,
+    w_up, bias_up, w_down, bias_down, cotangent,
+):
+    x = inputs[0]
+    tokens, width = x.shape
+    ff = w_up.shape[1]
+    halo = 256
+    ext = tokens + halo
+    heads = width // HEAD_DIM
+    steps = ff // 512
+    chunks = 2 * steps + 8
+    slopes = jnp.asarray(
+        np.broadcast_to((2.0 ** -(np.arange(heads) + 1.0) * LOG2E)[:, None], (heads, 128)).astype(np.float32)
+    )
+    shards = (
+        (width // 16, ff // 2), (ff // 16, width // 2), (width // 16, width // 2), (width // 16, 3 * width // 2),
+    )
+    out, gin, g_up, g_down, g_out, g_qkv, vec = pl.pallas_call(
+        functools.partial(layer_kernel, halo),
+        out_shape=(shape((tokens, width), BF16), shape((tokens, width), F32))
+        + tuple(shape(dims, BF16) for dims in shards)
+        + (shape((16, width), F32),),
+        in_specs=[vmem()] * 12 + [hbm()] * 5,
+        out_specs=(hbm(),) * 2 + (vmem(),) * 5,
+        scratch_shapes=[
+            pltpu.VMEM((ext, 3 * width), BF16),
+            pltpu.VMEM((width, ext), BF16),
+            pltpu.VMEM((width, tokens), BF16),
+            pltpu.VMEM((2, 512, 256), F32),
+            pltpu.VMEM((1, tokens), jnp.int32),
+            pltpu.VMEM((tokens, width), F32),
+            pltpu.VMEM((tokens, width), BF16),
+            pltpu.VMEM((tokens, width), BF16),
+            pltpu.VMEM((width, tokens), BF16),
+            pltpu.VMEM((ff, tokens), BF16),
+            pltpu.VMEM((tokens, 512), BF16),
+            pltpu.VMEM((tokens, width), F32),
+            pltpu.VMEM((tokens, width), F32),
+            pltpu.VMEM((halo, width), F32),
+            pltpu.VMEM((ext, 3 * width), BF16),
+            pltpu.VMEM((2, width, 512), BF16),
+            pltpu.VMEM((2, 512, width), BF16),
+            pltpu.VMEM((1, 3 * width), F32),
+            pltpu.VMEM((1, ff), F32),
+            pltpu.VMEM((RING, 2, 32, 32, 256), BF16),
+            pltpu.VMEM((chunks, 32, 32, 256), BF16),
+        ]
+        + arrival_shapes(chunks)
+        + [
+            pltpu.VMEM((5, 2, 16, width), F32),
+            DMA((6,)), DMA((2,)), DMA((2, 4)), DMA, DMA((RING,)), DMA((chunks,)), DMA((4, chunks, 2)),
+            DMA((4, chunks, 2)), DMA((3,)), DMA((3,)), DMA((5,)), DMA((5,)), DMA((2,)),
+        ],
+        compiler_params=params(0),
+        name="layer",
+    )(
+        x, doc_ids, slopes, bias_q, bias_v, bias_out, norm1_gain, norm1_bias, norm2_gain, norm2_bias, bias_up, bias_down,
+        cotangent[0], w_qkv, w_out, w_up, w_down,
+    )
+    row = shape((width,), F32)
+    return_shapes = (
+        shape((tokens, width), BF16), shape((tokens, width), F32), shape(shards[3], F32), row, row, shape(shards[2], F32),
+        row, row, row, row, row, shape(shards[0], F32), shape((ff,), F32), shape(shards[1], F32), row,
+    )
+    results = pl.pallas_call(
+        finish_kernel,
+        out_shape=return_shapes,
+        in_specs=[vmem()] * 7,
+        out_specs=(vmem(),) * 15,
+        name="hand_over",
+    )(out, gin, g_up, g_down, g_out, g_qkv, vec)
+    return (results[0][None], results[1][None]) + tuple(results[2:])
 
 
 def smooth_act(values):
@@ -361,4 +1140,6 @@
         P("dp", "seq"),
         P(),
     )
-    return jax.shard_map(local, mesh=mesh, in_specs=in_specs, out_specs=out_specs, check_vma=False)
+    sizes = (mesh.shape["dp"], mesh.shape["seq"])
+    chosen = fast_local if sizes == (16, 2) else local
+    return jax.shard_map(chosen, mesh=mesh, in_specs=in_specs, out_specs=out_specs, check_vma=False)

time: 845 us -> 163 us (0.19); the launches traced: 835 us -> 163 us
  waiting for transfers between devices: 325 us -> 0 us
  matrix products: 214 us -> 0 us
  Pallas kernels: 0 us -> 162 us
  local copies, waits for them, and re-layouts: 104 us -> 0 us
  other arithmetic: 56.2 us -> 0 us
  blocking collectives: 54.2 us -> 0 us
  starting transfers between devices: 33.6 us -> 0 us
  loops' own time: 33 us -> 0 us
  between operations: 15.4 us -> 0.86 us
    reduce_scatter x8 -> x0, waiting for transfers between devices: 263 us -> none  [the longest x1 98.8 us: local(): lax.psum_scatter(matrices[3].astype(jnp.bfloat16), 'dp', scatter_dimensio...]
    dot_general x68 -> x0, matrix products: 214 us -> none  [the longest x16 45.7 us: block_scores(): lax.dot_general(query_block, key_rows, (((1,), (1,)), ((), ())), preferre...]
    pallas_call x0 -> x2, Pallas kernels: none -> 162 us  [the longest x1 158 us: fast_local(): pl.pallas_call(functools.partial(layer_kernel, halo), out_shape=(shape((t...]
    all_to_all x8 -> x0, waiting for transfers between devices: 61.7 us -> none  [the longest x1 12.7 us: local(): lax.all_to_all(query_rows, 'seq', split_axis=1, concat_axis=0, tiled=True)]
    psum x1 -> x0, blocking collectives: 41.7 us -> none  [local(): lax.psum((g_bias_q, g_bias_v, g_bias_out, g_gain_one, g_shift_one, g_gain...]
    another operation x10 -> x0, loops' own time: 33 us -> none  [the longest x4 17 us: head_backward(): lax.scan(one_block, (zeros_block, zeros_block), starts)]
    all_to_all x8 -> x0, starting transfers between devices: 32.8 us -> none  [the longest x1 4.95 us: local(): lax.all_to_all(jnp.moveaxis(head_outs, 0, 1), 'seq', split_axis=0, concat...]
    squeeze x24 -> x0, local copies, waits for them, and re-layouts: 23.8 us -> none  [local(): lax.map(forward_head, (head_q, head_k, head_v, slopes))]
  transfers between devices with their start and end apart: 16 -> 0, of which waited for: 11 -> 0; matrix products, arithmetic and copies ran while one was open for 24% -> 0% of each run, Pallas kernels for 0% -> 0%
where the time goes in v2:
time: 163 us
  Pallas kernels  162 us (99%)
    pallas_call x1, Pallas kernels, fast_local(): pl.pallas_call(functools.partial(layer_kernel, halo), out_shape=(shape((t...  158 us
    pallas_call x1, Pallas kernels, fast_local(): pl.pallas_call(finish_kernel, out_shape=return_shapes, in_specs=[vmem()]...  4.4 us

profile of v2, /device:TPU:0, one launch (start us, length us, event | category | flops | bytes accessed | tf_op | source)
XLA Modules:
  0.0 162.8 jit_solution(15991000373161846180)
XLA Ops:
  0.7 157.6 %layer.1 = (bf16[512,1024]{1,0:T(8,128)(2,1)}, f32[512,1024]{1,0:T(8,128)}, bf16[64,2048]{1,0:T(8,128)(2,1)}, bf16[256,512]{1,0:T(8,128)(2,1)}, bf16[64,512]{1,0...) custom-call(bf16[512,1024]{1,0:T(8,128)(2,1)} %bitcast.4, s32[1,512]{1,0:T(1,128)} %doc_ref.1, ...), custom_call_target="tpu_custom_call" | custom-call | tf_op jit(solution)/shard_map/layer/pallas_call | solution.py:735
  158.2 4.4 %hand_over.1 = (bf16[512,1024]{1,0:T(8,128)(2,1)}, f32[512,1024]{1,0:T(8,128)}, f32[64,1536]{1,0:T(8,128)}, f32[1024]{0:T(1024)}, f32[1024]{0:T(1024)}, /*index=...) custom-call(bf16[512,1024]{1,0:T(8,128)(2,1)} %get-tuple-element.37., ...), custom_call_target="tpu_custom_call" | custom-call | tf_op jit(solution)/shard_map/hand_over/pallas_call | solution.py:782

commit v3 on v2

--- a/solution.py
+++ b/solution.py
@@ -66,9 +66,16 @@
 ORDERS = (("x", "a", "y", "b"), ("y", "a", "x", "b"))
 
 
-def block_index(half, place):
+ALONG_X = (18, 20, 22)
+
+
+def order_of(chunk, half):
+    return ORDERS[0 if isinstance(chunk, int) and chunk in ALONG_X else half]
+
+
+def block_index(chunk, half, place):
     index = half * 16
-    for kind, weight in zip(ORDERS[half], (8, 4, 2, 1)):
+    for kind, weight in zip(order_of(chunk, half), (8, 4, 2, 1)):
         index = index + place[kind] * weight
     return index
 
@@ -83,10 +90,10 @@
         self.send_sem, self.recv_sem = send_sem, recv_sem
         self.me = coords()
 
-    def offset(self, half, stage, other):
+    def offset(self, chunk, half, stage, other):
         index = half * 16
         for k, weight in zip(range(stage + 1), (8, 4, 2, 1)):
-            bit = self.me[ORDERS[half][k]]
+            bit = self.me[order_of(chunk, half)[k]]
             if other and k == stage:
                 bit = 1 - bit
             index = index + bit * weight
@@ -95,11 +102,11 @@
     def copy(self, chunk, stage, half):
         size = 8 >> stage
         return pltpu.make_async_remote_copy(
-            src_ref=self.held.at[chunk, pl.ds(self.offset(half, stage, True), size)],
+            src_ref=self.held.at[chunk, pl.ds(self.offset(chunk, half, stage, True), size)],
             dst_ref=self.arrivals[stage].at[chunk, half],
             send_sem=self.send_sem.at[stage, chunk, half],
             recv_sem=self.recv_sem.at[stage, chunk, half],
-            device_id=partner(ORDERS[half][stage]),
+            device_id=partner(order_of(chunk, half)[stage]),
             device_id_type=MESH,
         )
 
@@ -111,11 +118,11 @@
         size = 8 >> stage
         for half in range(2):
             self.copy(chunk, stage, half).wait()
-            mine = pl.ds(self.offset(half, stage, False), size)
+            mine = pl.ds(self.offset(chunk, half, stage, False), size)
             self.held[chunk, mine] = self.held[chunk, mine] + self.arrivals[stage][chunk, half]
 
     def result(self, chunk, half):
-        return self.held[chunk, self.offset(half, 3, False)]
+        return self.held[chunk, self.offset(chunk, half, 3, False)]
 
 
 def arrival_shapes(chunks):
@@ -137,7 +144,7 @@
 
 
 RING = 3
-AHEAD = 3
+AHEAD = 2
 
 
 def row_of(ref):
@@ -229,7 +236,7 @@
             place["y"] = yy
             for h in range(2):
                 r0 = q * 64 + h * 32
-                grad[n % RING, place["c"], block_index(h, place)] = tile[r0 : r0 + 32].astype(BF16)
+                grad[n % RING, place["c"], block_index(n, h, place)] = tile[r0 : r0 + 32].astype(BF16)
 
     def store(n):
         for h in range(2):
@@ -316,16 +323,19 @@
             for u in range(FWD_HEADS):
                 h = i * FWD_HEADS + u
                 c0 = pl.multiple_of(h * HEAD_DIM, HEAD_DIM)
-                q = qkv[halo + block * 256 : halo + (block + 1) * 256, pl.ds(c0, HEAD_DIM)]
-                k = qkv[block * 256 : block * 256 + 512, pl.ds(width + c0, HEAD_DIM)]
-                v = qkv[block * 256 : block * 256 + 512, pl.ds(2 * width + c0, HEAD_DIM)]
                 slope = slope_ref[pl.ds(h, 1), 0:1]
-                s = dot_nt(k, q) * (LOG2E * scale) - slope * dist[block]
-                e = jnp.exp2(s - jnp.max(s, axis=0, keepdims=True))
-                p = (e * (1.0 / jnp.sum(e, axis=0, keepdims=True))).astype(BF16)
-                o_t = dot_tn(v, p)
-                ot[pl.ds(c0, HEAD_DIM), block * 256 : (block + 1) * 256] = o_t.astype(BF16)
-                o_s[block * 256 : (block + 1) * 256, pl.ds(c0, HEAD_DIM)] = o_t.T.astype(BF16)
+                for t in range(2):
+                    row = block * 256 + t * 128
+                    q = qkv[halo + row : halo + row + 128, pl.ds(c0, HEAD_DIM)]
+                    k = qkv[row : row + 384, pl.ds(width + c0, HEAD_DIM)]
+                    v = qkv[row : row + 384, pl.ds(2 * width + c0, HEAD_DIM)]
+                    far = dist[block, t * 128 : t * 128 + 384, t * 128 : t * 128 + 128]
+                    s = dot_nt(k, q) * (LOG2E * scale) - slope * far
+                    e = jnp.exp2(s - jnp.max(s, axis=0, keepdims=True))
+                    p = (e * (1.0 / jnp.sum(e, axis=0, keepdims=True))).astype(BF16)
+                    o_t = dot_tn(v, p)
+                    ot[pl.ds(c0, HEAD_DIM), row : row + 128] = o_t.astype(BF16)
+                    o_s[row : row + 128, pl.ds(c0, HEAD_DIM)] = o_t.T.astype(BF16)
             return carry
 
         lax.fori_loop(0, heads // FWD_HEADS, some_heads, 0)
@@ -389,6 +399,13 @@
                 cp.start()
 
         for yy in range(2):
+            if yy == 1:
+
+                @pl.when(f >= 1)
+                def _():
+                    join(f - 1)
+                    scatter.start(f - 1, 0)
+
             cols = slice(yy * 256, (yy + 1) * 256)
             first = pl.multiple_of(yy * half_ff + f * 256, 256)
             shift = bup[:, pl.ds(first, 256)]
@@ -398,21 +415,16 @@
                 u = dot(act2[rows], wu[slot, :, cols]) + shift
                 dh = dot_nt(cot[rows], wd[slot, cols])
                 uu = u * u
-                th = jnp.tanh(GELU_C * u * (1.0 + GELU_A * uu))
-                half_u = 0.5 * u
-                hv = (half_u * (1.0 + th)).astype(BF16)
-                slope = 0.5 * (1.0 + th) + half_u * (1.0 - th * th) * (GELU_C * (1.0 + 3.0 * GELU_A * uu))
+                gate = 0.5 * jnp.tanh(u * (GELU_C + GELU_C * GELU_A * uu)) + 0.5
+                act = u * gate
+                hv = act.astype(BF16)
+                slope = gate + act * (1.0 - gate) * (2.0 * GELU_C + 6.0 * GELU_C * GELU_A * uu)
                 dv = (dh * slope).astype(BF16)
                 dpre[rows, cols] = dv
                 hid_t[pl.ds(first, 256), rows] = hv.T
                 sums = sums + jnp.sum(dv.astype(F32), axis=0, keepdims=True)
             row = yy * (half_ff // width) + f // (width // 256)
             vec[pl.ds(8 + row, 1), pl.ds(pl.multiple_of((f % (width // 256)) * 256, 256), 256)] = sums
-
-        @pl.when(f >= 1)
-        def _():
-            join(f - 1)
-            scatter.start(f - 1, 0)
 
         for yy in range(2):
             cols = slice(yy * 256, (yy + 1) * 256)
@@ -422,7 +434,7 @@
         for m in range(tokens // 256):
             rows = slice(m * 256, (m + 1) * 256)
             dn2[rows] += dot_nt(dpre[rows], wu[slot])
-        service(f - 3, ahead=False)
+        service(f - 2, ahead=False)
         return carry
 
     lax.fori_loop(0, steps, ff_step, 0)
@@ -456,7 +468,7 @@
         def _():
             join(n - 1)
 
-        for at, t in ((2, steps - 3), (5, steps - 2), (7, steps - 1)):
+        for at, t in ((2, steps - 2), (5, steps - 1), (7, steps)):
 
             @pl.when(i == at)
             def _(t=t):
@@ -488,7 +500,7 @@
 
     lax.fori_loop(0, tokens // 64, norm_two, 0)
     dx2, ab, do = dn2, cot, act2
-    service(steps)
+    service(steps + 1)
 
     for j in range(2):
         for yy in range(2):
@@ -496,7 +508,7 @@
             for m in range(width // 256):
                 put(first_out + j, yy, m, dot(ot[m * 256 : (m + 1) * 256], ab[:, c0 : c0 + 256]))
         core_copy(first_out + j).start()
-    service(steps + 1)
+    service(steps + 2)
     for cp in oloads:
         cp.wait()
     for m in range(tokens // 256):
@@ -511,9 +523,10 @@
     dload(1).start()
     join(first_out)
     join(first_out + 1)
-    service(steps + 2)
+    service(steps + 3)
 
     dqkv[0:halo, 0:width] = jnp.zeros((halo, width), BF16)
+    act2t[...] = jnp.zeros(act2t.shape, BF16)
 
     def head_back(h):
         c0 = pl.multiple_of(h * HEAD_DIM, HEAD_DIM)
@@ -524,16 +537,25 @@
             krows = slice(block * 256, block * 256 + 512)
             q = qkv[rows, pl.ds(c0, HEAD_DIM)]
             k = qkv[krows, pl.ds(width + c0, HEAD_DIM)]
-            v = qkv[krows, pl.ds(2 * width + c0, HEAD_DIM)]
             g = do[block * 256 : (block + 1) * 256, pl.ds(c0, HEAD_DIM)]
-            s = dot_nt(k, q) * (LOG2E * scale) - slope * dist[block]
-            e = jnp.exp2(s - jnp.max(s, axis=0, keepdims=True))
-            p = e * (1.0 / jnp.sum(e, axis=0, keepdims=True))
-            dp = dot_nt(v, g)
-            delta = jnp.sum(p * dp, axis=0, keepdims=True)
-            ds = (p * (dp - delta)).astype(BF16)
-            dqkv[rows, pl.ds(c0, HEAD_DIM)] = (dot_tn(ds, k) * scale).astype(BF16)
-            parts.append((dot(ds, q) * scale, dot(p.astype(BF16), g)))
+            for t in range(2):
+                row = block * 256 + t * 128
+                keys, cols = slice(t * 128, t * 128 + 384), slice(t * 128, t * 128 + 128)
+                qs = qkv[halo + row : halo + row + 128, pl.ds(c0, HEAD_DIM)]
+                ks = qkv[row : row + 384, pl.ds(width + c0, HEAD_DIM)]
+                vs = qkv[row : row + 384, pl.ds(2 * width + c0, HEAD_DIM)]
+                s = dot_nt(ks, qs) * (LOG2E * scale) - slope * dist[block, keys, cols]
+                e = jnp.exp2(s - jnp.max(s, axis=0, keepdims=True))
+                p = e * (1.0 / jnp.sum(e, axis=0, keepdims=True))
+                dp = dot_nt(vs, do[row : row + 128, pl.ds(c0, HEAD_DIM)])
+                delta = jnp.sum(p * dp, axis=0, keepdims=True)
+                keys = slice(block * 512 + t * 128, block * 512 + t * 128 + 384)
+                act2t[keys, cols] = p.astype(BF16)
+                act2t[keys, 256 + t * 128 : 384 + t * 128] = (p * (dp - delta)).astype(BF16)
+            both = slice(block * 512, (block + 1) * 512)
+            pb, ds = act2t[both, 0:256], act2t[both, 256:512]
+            dqkv[rows, pl.ds(c0, HEAD_DIM)] = (dot_tn(k, ds) * scale).T.astype(BF16)
+            parts.append((dot(ds, q) * scale, dot(pb, g)))
         for which in range(2):
             cols = pl.ds((1 + which) * width + c0, HEAD_DIM)
             first, second = parts[0][which], parts[1][which]
@@ -544,14 +566,46 @@
     def heads_back(i, carry):
         for u in range(2):
             head_back(i * 2 + u)
-        service(steps + 3 + i)
+        service(steps + 4 + i)
         return carry
 
     lax.fori_loop(0, heads // 2, heads_back, 0)
     vec[0:1] = jnp.sum(dqkv[halo:, 0:width].astype(F32), axis=0, keepdims=True)
     vec[1:2] = jnp.sum(dqkv[:, 2 * width :].astype(F32), axis=0, keepdims=True)
 
-    t0 = steps + 3 + heads // 2
+    state = {"t": steps + 4 + heads // 2}
+
+    def serve():
+        if state["t"] < chunks + 6:
+            service(state["t"])
+            state["t"] += 1
+
+    back = pltpu.make_async_remote_copy(
+        src_ref=dn_send, dst_ref=dn_come, send_sem=hs.at[2], recv_sem=hr.at[2],
+        device_id=partner("y"), device_id_type=MESH,
+    )
+
+    def dn_part(i):
+        cols = slice(order[i] * 512, (order[i] + 1) * 512)
+        qload(i).wait()
+        if i < 4:
+            part = dot_nt(dqkv[0:halo, cols], wu[i % 2])
+            if i == 0:
+                dnh[...] = part
+            elif i < 3:
+                dnh[...] += part
+            else:
+                dn_send[...] = (dnh[...] + part).astype(BF16)
+        for m in range(tokens // 256):
+            rows = slice(m * 256, (m + 1) * 256)
+            part = dot_nt(dqkv[halo + m * 256 : halo + (m + 1) * 256, cols], wu[i % 2])
+            if i == 0:
+                dn1[rows] = part
+            else:
+                dn1[rows] += part
+        if i + 2 < 6:
+            qload(i + 2).start()
+
     for j in range(6):
         n = first_qkv + j
         for yy in range(2):
@@ -562,41 +616,20 @@
         if j >= 1:
             join(n - 1)
         if j % 2 == 1:
-            service(t0)
-            t0 += 1
-    join(chunks - 1)
-
-    for i, j in enumerate(order):
-        qload(i).wait()
-        cols = slice(j * 512, (j + 1) * 512)
-        if i < 4:
-            part = dot_nt(dqkv[0:halo, cols], wu[i % 2])
-            if i == 0:
-                dnh[...] = part
-            else:
-                dnh[...] += part
-        for m in range(tokens // 256):
-            part = dot_nt(dqkv[halo + m * 256 : halo + (m + 1) * 256, cols], wu[i % 2])
-            if i == 0:
-                dn1[m * 256 : (m + 1) * 256] = part
-            else:
-                dn1[m * 256 : (m + 1) * 256] += part
-        if i + 2 < 6:
-            qload(i + 2).start()
-        if i == 3:
-            dn_send[...] = dnh[...].astype(BF16)
-            back = pltpu.make_async_remote_copy(
-                src_ref=dn_send, dst_ref=dn_come, send_sem=hs.at[2], recv_sem=hr.at[2],
-                device_id=partner("y"), device_id_type=MESH,
-            )
+            serve()
+        if j == 3:
+            for i in range(4):
+                dn_part(i)
 
             @pl.when(seq == 1)
             def _():
                 back.start()
 
-        if i % 2 == 1:
-            service(t0)
-            t0 += 1
+            serve()
+    join(chunks - 1)
+    for i in (4, 5):
+        dn_part(i)
+    serve()
 
     def out_part(i):
         dload(i).wait()
@@ -612,10 +645,9 @@
         if i + 2 < 8:
             dload(i + 2).start()
 
-    for i in range(4):
+    for i in range(3):
         out_part(i)
-    service(t0)
-    t0 += 1
+    serve()
 
     @pl.when(seq == 1)
     def _():
@@ -655,12 +687,17 @@
 
     vin[0, 0] = vec[...]
     vec_copy(0).start()
+    save_out = pltpu.make_async_copy(act2, out_hbm, esem.at[1])
     for i in range(5):
-        if i < 4:
-            out_part(4 + i)
-        if t0 < chunks:
-            service(t0)
-            t0 += 1
+        serve()
+        if i == 0:
+            out_part(3)
+            out_part(4)
+            out_part(5)
+        if i == 1:
+            out_part(6)
+            out_part(7)
+            save_out.start()
         vec_copy(i).wait()
         total = vin[i, 0] + vin[i, 1]
         if i < 4:
@@ -668,11 +705,8 @@
             vec_copy(i + 1).start()
         else:
             vec[...] = total
-        if i == 3:
-            save_out = pltpu.make_async_copy(act2, out_hbm, esem.at[1])
-            save_out.start()
-    for t in range(t0, chunks + 6):
-        service(t)
+    while state["t"] < chunks + 6:
+        serve()
     save_gin.wait()
     save_out.wait()
 

time: 163 us -> 150 us (0.920)
  Pallas kernels: 162 us -> 149 us
    pallas_call x1, Pallas kernels: 158 us -> 144 us  [fast_local(): pl.pallas_call(functools.partial(layer_kernel, halo), out_shape=(shape((t...]
where the time goes in v3:
time: 150 us
  Pallas kernels  149 us (99%)
    pallas_call x1, Pallas kernels, fast_local(): pl.pallas_call(functools.partial(layer_kernel, halo), out_shape=(shape((t...  144 us
    pallas_call x1, Pallas kernels, fast_local(): pl.pallas_call(finish_kernel, out_shape=return_shapes, in_specs=[vmem()]...  4.4 us

profile of v3, /device:TPU:0, one launch (start us, length us, event | category | flops | bytes accessed | tf_op | source)
XLA Modules:
  0.0 149.5 jit_solution(5127856525719704068)
XLA Ops:
  0.7 144.3 %layer.1 = (bf16[512,1024]{1,0:T(8,128)(2,1)}, f32[512,1024]{1,0:T(8,128)}, bf16[64,2048]{1,0:T(8,128)(2,1)}, bf16[256,512]{1,0:T(8,128)(2,1)}, bf16[64,512]{1,0...) custom-call(bf16[512,1024]{1,0:T(8,128)(2,1)} %bitcast.4, s32[1,512]{1,0:T(1,128)} %doc_ref.1, ...), custom_call_target="tpu_custom_call" | custom-call | tf_op jit(solution)/shard_map/layer/pallas_call | solution.py:769
  144.9 4.4 %hand_over.1 = (bf16[512,1024]{1,0:T(8,128)(2,1)}, f32[512,1024]{1,0:T(8,128)}, f32[64,1536]{1,0:T(8,128)}, f32[1024]{0:T(1024)}, f32[1024]{0:T(1024)}, /*index=...) custom-call(bf16[512,1024]{1,0:T(8,128)(2,1)} %get-tuple-element.37., ...), custom_call_target="tpu_custom_call" | custom-call | tf_op jit(solution)/shard_map/hand_over/pallas_call | solution.py:816

commit v4 on v3

--- a/solution.py
+++ b/solution.py
@@ -104,8 +104,8 @@
         return pltpu.make_async_remote_copy(
             src_ref=self.held.at[chunk, pl.ds(self.offset(chunk, half, stage, True), size)],
             dst_ref=self.arrivals[stage].at[chunk, half],
-            send_sem=self.send_sem.at[stage, chunk, half],
-            recv_sem=self.recv_sem.at[stage, chunk, half],
+            send_sem=self.send_sem.at[stage],
+            recv_sem=self.recv_sem.at[stage, chunk],
             device_id=partner(order_of(chunk, half)[stage]),
             device_id_type=MESH,
         )
@@ -114,10 +114,20 @@
         for half in range(2):
             self.copy(chunk, stage, half).start()
 
+    def whole(self, stage, ref, at):
+        return pltpu.make_async_remote_copy(
+            src_ref=ref, dst_ref=ref, send_sem=self.send_sem.at[stage], recv_sem=self.recv_sem.at[stage, at],
+            device_id=partner("x"), device_id_type=MESH,
+        )
+
+    def sent(self):
+        for stage in range(4):
+            self.whole(stage, self.arrivals[stage], 0).wait_send()
+
     def finish(self, chunk, stage):
         size = 8 >> stage
+        self.whole(stage, self.arrivals[stage].at[chunk], chunk).wait_recv()
         for half in range(2):
-            self.copy(chunk, stage, half).wait()
             mine = pl.ds(self.offset(chunk, half, stage, False), size)
             self.held[chunk, mine] = self.held[chunk, mine] + self.arrivals[stage][chunk, half]
 
@@ -292,17 +302,22 @@
     bias[:, 2 * width :] = row_of(bv_ref)
     bup[...] = row_of(bup_ref)
 
-    for r in range(tokens // 128):
-        v = norm(x_ref[r * 128 : (r + 1) * 128].astype(F32), gain1, shift1).astype(BF16)
-        act1[halo + r * 128 : halo + (r + 1) * 128] = v
-        act1t[:, halo + r * 128 : halo + (r + 1) * 128] = v.T
-
-    for j in range(6):
-        qloads[j].wait()
-        cols = slice(j * 512, (j + 1) * 512)
-        for m in range(tokens // 256):
-            rows = slice(halo + m * 256, halo + (m + 1) * 256)
+    def norm_rows(m):
+        for r in range(2 * m, 2 * m + 2):
+            v = norm(x_ref[r * 128 : (r + 1) * 128].astype(F32), gain1, shift1).astype(BF16)
+            act1[halo + r * 128 : halo + (r + 1) * 128] = v
+            act1t[:, halo + r * 128 : halo + (r + 1) * 128] = v.T
+
+    norm_rows(0)
+    for cp in qloads:
+        cp.wait()
+    for m in range(tokens // 256):
+        rows = slice(halo + m * 256, halo + (m + 1) * 256)
+        for j in range(6):
+            cols = slice(j * 512, (j + 1) * 512)
             qkv[rows, cols] = (dot(act1[rows], wqkv_part(j)[...]) + bias[:, cols]).astype(BF16)
+            if m == 0 and j == 0:
+                norm_rows(1)
     for cp in weights(0, 0):
         cp.start()
 
@@ -707,6 +722,7 @@
             vec[...] = total
     while state["t"] < chunks + 6:
         serve()
+    scatter.sent()
     save_gin.wait()
     save_out.wait()
 
@@ -726,7 +742,7 @@
         b_up[i * width : (i + 1) * width] = vec[8 + i]
 
 
-FWD_HEADS = 2
+FWD_HEADS = 4
 
 
 def vmem():
@@ -799,8 +815,8 @@
         + arrival_shapes(chunks)
         + [
             pltpu.VMEM((5, 2, 16, width), F32),
-            DMA((6,)), DMA((2,)), DMA((2, 4)), DMA, DMA((RING,)), DMA((chunks,)), DMA((4, chunks, 2)),
-            DMA((4, chunks, 2)), DMA((3,)), DMA((3,)), DMA((5,)), DMA((5,)), DMA((2,)),
+            DMA((6,)), DMA((2,)), DMA((2, 4)), DMA, DMA((RING,)), DMA((chunks,)), DMA((4,)),
+            DMA((4, chunks)), DMA((3,)), DMA((3,)), DMA((5,)), DMA((5,)), DMA((2,)),
         ],
         compiler_params=params(0),
         name="layer",

time: 150 us -> 147 us (0.980)
  Pallas kernels: 149 us -> 146 us
    pallas_call x1, Pallas kernels: 144 us -> 141 us  [fast_local(): pl.pallas_call(functools.partial(layer_kernel, halo), out_shape=(shape((t...]
where the time goes in v4:
time: 147 us; the launch traced here: 146 us
  Pallas kernels  146 us (99%)
    pallas_call x1, Pallas kernels, fast_local(): pl.pallas_call(functools.partial(layer_kernel, halo), out_shape=(shape((t...  141 us
    pallas_call x1, Pallas kernels, fast_local(): pl.pallas_call(finish_kernel, out_shape=return_shapes, in_specs=[vmem()]...  4.4 us

profile of v4, /device:TPU:0, one launch (start us, length us, event | category | flops | bytes accessed | tf_op | source)
XLA Modules:
  0.0 146.4 jit_solution(6502372733428703971)
XLA Ops:
  0.7 141.1 %layer.1 = (bf16[512,1024]{1,0:T(8,128)(2,1)}, f32[512,1024]{1,0:T(8,128)}, bf16[64,2048]{1,0:T(8,128)(2,1)}, bf16[256,512]{1,0:T(8,128)(2,1)}, bf16[64,512]{1,0...) custom-call(bf16[512,1024]{1,0:T(8,128)(2,1)} %bitcast.4, s32[1,512]{1,0:T(1,128)} %doc_ref.1, ...), custom_call_target="tpu_custom_call" | custom-call | tf_op jit(solution)/shard_map/layer/pallas_call | solution.py:785
  141.8 4.4 %hand_over.1 = (bf16[512,1024]{1,0:T(8,128)(2,1)}, f32[512,1024]{1,0:T(8,128)}, f32[64,1536]{1,0:T(8,128)}, f32[1024]{0:T(1024)}, f32[1024]{0:T(1024)}, /*index=...) custom-call(bf16[512,1024]{1,0:T(8,128)(2,1)} %get-tuple-element.37., ...), custom_call_target="tpu_custom_call" | custom-call | tf_op jit(solution)/shard_map/hand_over/pallas_call | solution.py:832

commit v5 on v4

--- a/solution.py
+++ b/solution.py
@@ -162,12 +162,14 @@
 
 
 def layer_kernel(
-    halo, x_ref, doc_ref, slope_ref, bq_ref, bv_ref, bo_ref, g1_ref, s1_ref, g2_ref, s2_ref, bup_ref, bdown_ref,
+    halo, x_hbm, doc_hbm, slope_hbm, bq_hbm, bv_hbm, bo_hbm, g1_hbm, s1_hbm, g2_hbm, s2_hbm, bup_hbm, bdown_hbm,
     cot_hbm, wqkv_hbm, wout_hbm, wup_hbm, wdown_hbm,
-    out_hbm, gin_hbm, gup, gdown, gout, gqkv, vec,
+    out_hbm, gin_hbm, gup_hbm, gdown_hbm, gout_hbm, gqkv_hbm, vec_hbm,
+    gup, gdown, gout, gqkv, vec,
+    x_ref, doc_ref, slope_ref, bq_ref, bv_ref, bo_ref, g1_ref, s1_ref, g2_ref, s2_ref, bup_ref, bdown_ref,
     qkv, act1t, ot, dist, doch, x2, cot, act2, act2t, hid_t, dpre, dn2, dn1, dnh, dqkv, wu, wd, bias, bup,
     grad, held, r1, r2, r3, r4, vin,
-    qsem, osem, wsem, csem, cs, cr, ss, rs, hs, hr, vs, vr, esem,
+    rsem, isem, qsem, osem, wsem, csem, cs, cr, ss, rs, hs, hr, vs, vr, esem,
 ):
     tokens, width = x_ref.shape
     heads = width // HEAD_DIM
@@ -198,22 +200,41 @@
         pltpu.make_async_copy(wout_hbm.at[pl.ds(512, 512)], wd.at[1], osem.at[1]),
     ]
     cload = pltpu.make_async_copy(cot_hbm, cot, csem)
-    for cp in qloads + oloads + [cload]:
+    iloads = [
+        pltpu.make_async_copy(src, dst, isem.at[i])
+        for i, (src, dst) in enumerate(
+            (
+                (x_hbm, x_ref), (g1_hbm, g1_ref), (s1_hbm, s1_ref), (bq_hbm, bq_ref), (bv_hbm, bv_ref),
+                (doc_hbm, doc_ref), (slope_hbm, slope_ref), (bo_hbm, bo_ref), (g2_hbm, g2_ref), (s2_hbm, s2_ref),
+                (bup_hbm, bup_ref), (bdown_hbm, bdown_ref),
+            )
+        )
+    ]
+    for cp in iloads + qloads + oloads + [cload]:
         cp.start()
     greet(("c", "x", "a", "b", "y"))
-    send_x = pltpu.make_async_remote_copy(
-        src_ref=x_ref.at[pl.ds(tokens - halo, halo)], dst_ref=xh, send_sem=hs.at[0], recv_sem=hr.at[0],
-        device_id=partner("y"), device_id_type=MESH,
-    )
+    part_rows = halo // 2
+    send_x = [
+        pltpu.make_async_remote_copy(
+            src_ref=x_hbm.at[pl.ds(tokens - halo + (1 - i) * part_rows, part_rows)],
+            dst_ref=xh.at[pl.ds((1 - i) * part_rows, part_rows)], send_sem=hs.at[i], recv_sem=hr.at[i],
+            device_id=partner("y"), device_id_type=MESH,
+        )
+        for i in range(2)
+    ]
     send_doc = pltpu.make_async_remote_copy(
-        src_ref=doc_ref, dst_ref=doch, send_sem=hs.at[1], recv_sem=hr.at[1],
+        src_ref=doc_hbm, dst_ref=doch, send_sem=hs.at[3], recv_sem=hr.at[3],
         device_id=partner("y"), device_id_type=MESH,
     )
 
     @pl.when(seq == 0)
     def _():
         send_doc.start()
-        send_x.start()
+        for cp in send_x:
+            cp.start()
+
+    for cp in iloads:
+        cp.wait()
 
     def weights(f, slot):
         col = pl.multiple_of(f * 256, 256)
@@ -308,16 +329,14 @@
             act1[halo + r * 128 : halo + (r + 1) * 128] = v
             act1t[:, halo + r * 128 : halo + (r + 1) * 128] = v.T
 
-    norm_rows(0)
-    for cp in qloads:
-        cp.wait()
     for m in range(tokens // 256):
-        rows = slice(halo + m * 256, halo + (m + 1) * 256)
-        for j in range(6):
-            cols = slice(j * 512, (j + 1) * 512)
+        norm_rows(m)
+    for j in range(6):
+        qloads[j].wait()
+        cols = slice(j * 512, (j + 1) * 512)
+        for m in range(tokens // 256):
+            rows = slice(halo + m * 256, halo + (m + 1) * 256)
             qkv[rows, cols] = (dot(act1[rows], wqkv_part(j)[...]) + bias[:, cols]).astype(BF16)
-            if m == 0 and j == 0:
-                norm_rows(1)
     for cp in weights(0, 0):
         cp.start()
 
@@ -333,13 +352,13 @@
         allowed = (gap >= 0) & (keys == queries)
         dist[block] = jnp.where(allowed, gap.astype(F32), FAR)
 
-    def attend(block):
+    def attend(block, which):
         def some_heads(i, carry):
             for u in range(FWD_HEADS):
                 h = i * FWD_HEADS + u
                 c0 = pl.multiple_of(h * HEAD_DIM, HEAD_DIM)
                 slope = slope_ref[pl.ds(h, 1), 0:1]
-                for t in range(2):
+                for t in which:
                     row = block * 256 + t * 128
                     q = qkv[halo + row : halo + row + 128, pl.ds(c0, HEAD_DIM)]
                     k = qkv[row : row + 384, pl.ds(width + c0, HEAD_DIM)]
@@ -355,8 +374,8 @@
 
         lax.fori_loop(0, heads // FWD_HEADS, some_heads, 0)
 
-    def project(block):
-        for r in range(2):
+    def project(block, which):
+        for r in which:
             rows = slice(block * 256 + r * 128, block * 256 + (r + 1) * 128)
             second = (
                 x_ref[rows].astype(F32) + dot(o_s[rows, 0:512], wout_low[...]) + dot(o_s[rows, 512:1024], wd[1])
@@ -367,15 +386,16 @@
             act2t[:, rows] = v.T
 
     distances(1, jnp.concatenate([jnp.full((halo, 1), -1.0, F32), own_cols], axis=0))
-    attend(1)
+    attend(1, (0, 1))
     for cp in oloads:
         cp.wait()
-    project(1)
+    project(1, (0, 1))
 
     @pl.when(seq == 0)
     def _():
         send_doc.wait_send()
-        send_x.wait_send()
+        for cp in send_x:
+            cp.wait_send()
         doch[...] = jnp.full(doch.shape, -1, jnp.int32)
         act1t[:, 0:halo] = jnp.zeros((width, halo), BF16)
         qkv[0:halo, width:] = jnp.zeros((halo, 2 * width), BF16)
@@ -383,20 +403,25 @@
     @pl.when(seq == 1)
     def _():
         send_doc.wait_recv()
-        send_x.wait_recv()
-        for r in range(halo // 128):
-            v = norm(xh[r * 128 : (r + 1) * 128].astype(F32), gain1, shift1).astype(BF16)
-            act1[r * 128 : (r + 1) * 128] = v
-            act1t[:, r * 128 : (r + 1) * 128] = v.T
-        for j in range(2, 6):
-            cols = slice(j * 512, (j + 1) * 512)
-            qkv[0:halo, cols] = (dot(act1[0:halo], wqkv_part(j)[...]) + bias[:, cols]).astype(BF16)
 
     halo_doc = doch[...].astype(F32)[:, tokens - halo :]
     halo_cols = jnp.transpose(jnp.broadcast_to(halo_doc, (128, halo)))[:, 0:1]
     distances(0, jnp.concatenate([halo_cols, own_cols], axis=0))
-    attend(0)
-    project(0)
+    for i in range(2):
+        rows = slice((1 - i) * part_rows, (2 - i) * part_rows)
+
+        @pl.when(seq == 1)
+        def _(i=i, rows=rows):
+            send_x[i].wait_recv()
+            v = norm(xh[rows].astype(F32), gain1, shift1).astype(BF16)
+            act1[rows] = v
+            act1t[:, rows] = v.T
+            for j in range(2, 6):
+                cols = slice(j * 512, (j + 1) * 512)
+                qkv[rows, cols] = (dot(act1[rows], wqkv_part(j)[...]) + bias[:, cols]).astype(BF16)
+
+        attend(0, (1 - i,))
+        project(0, (1 - i,))
 
     cload.wait()
     vec[...] = jnp.zeros(vec.shape, F32)
@@ -630,9 +655,9 @@
         core_copy(n).start()
         if j >= 1:
             join(n - 1)
-        if j % 2 == 1:
+        if j in SERVE_AT:
             serve()
-        if j == 3:
+        if j == BACK_AT:
             for i in range(4):
                 dn_part(i)
 
@@ -662,7 +687,8 @@
 
     for i in range(3):
         out_part(i)
-    serve()
+    for _ in range(N1_AFTER):
+        serve()
 
     @pl.when(seq == 1)
     def _():
@@ -704,7 +730,8 @@
     vec_copy(0).start()
     save_out = pltpu.make_async_copy(act2, out_hbm, esem.at[1])
     for i in range(5):
-        serve()
+        for _ in range(VEC_SERVES[i]):
+            serve()
         if i == 0:
             out_part(3)
             out_part(4)
@@ -722,7 +749,17 @@
             vec[...] = total
     while state["t"] < chunks + 6:
         serve()
+    saves = [
+        pltpu.make_async_copy(src, dst, rsem.at[i])
+        for i, (src, dst) in enumerate(
+            ((gup, gup_hbm), (gdown, gdown_hbm), (gout, gout_hbm), (gqkv, gqkv_hbm), (vec, vec_hbm))
+        )
+    ]
+    for cp in saves:
+        cp.start()
     scatter.sent()
+    for cp in saves:
+        cp.wait()
     save_gin.wait()
     save_out.wait()
 
@@ -743,6 +780,10 @@
 
 
 FWD_HEADS = 4
+BACK_AT = 3
+SERVE_AT = (1, 3, 5)
+N1_AFTER = 1
+VEC_SERVES = (1, 1, 1, 1, 1)
 
 
 def vmem():
@@ -787,9 +828,14 @@
         out_shape=(shape((tokens, width), BF16), shape((tokens, width), F32))
         + tuple(shape(dims, BF16) for dims in shards)
         + (shape((16, width), F32),),
-        in_specs=[vmem()] * 12 + [hbm()] * 5,
-        out_specs=(hbm(),) * 2 + (vmem(),) * 5,
-        scratch_shapes=[
+        in_specs=[hbm()] * 17,
+        out_specs=(hbm(),) * 7,
+        scratch_shapes=[pltpu.VMEM(dims, BF16) for dims in shards]
+        + [pltpu.VMEM((16, width), F32)]
+        + [pltpu.VMEM((tokens, width), BF16), pltpu.VMEM((1, tokens), jnp.int32), pltpu.VMEM((heads, 128), F32)]
+        + [pltpu.VMEM((width,), BF16)] * 7
+        + [pltpu.VMEM((ff,), BF16), pltpu.VMEM((width,), BF16)]
+        + [
             pltpu.VMEM((ext, 3 * width), BF16),
             pltpu.VMEM((width, ext), BF16),
             pltpu.VMEM((width, tokens), BF16),
@@ -815,8 +861,8 @@
         + arrival_shapes(chunks)
         + [
             pltpu.VMEM((5, 2, 16, width), F32),
-            DMA((6,)), DMA((2,)), DMA((2, 4)), DMA, DMA((RING,)), DMA((chunks,)), DMA((4,)),
-            DMA((4, chunks)), DMA((3,)), DMA((3,)), DMA((5,)), DMA((5,)), DMA((2,)),
+            DMA((5,)), DMA((12,)), DMA((6,)), DMA((2,)), DMA((2, 4)), DMA, DMA((RING,)), DMA((chunks,)), DMA((4,)),
+            DMA((4, chunks)), DMA((4,)), DMA((4,)), DMA((5,)), DMA((5,)), DMA((2,)),
         ],
         compiler_params=params(0),
         name="layer",

time: 147 us -> 144 us (0.980)
  Pallas kernels: 146 us -> 143 us
    pallas_call x1, Pallas kernels: 141 us -> 138 us  [fast_local(): pl.pallas_call(functools.partial(layer_kernel, halo), out_shape=(shape((t...]
where the time goes in v5:
time: 144 us; the launch traced here: 143 us
  Pallas kernels  143 us (99%)
    pallas_call x1, Pallas kernels, fast_local(): pl.pallas_call(functools.partial(layer_kernel, halo), out_shape=(shape((t...  138 us
    pallas_call x1, Pallas kernels, fast_local(): pl.pallas_call(finish_kernel, out_shape=return_shapes, in_specs=[vmem()]...  4.4 us

profile of v5, /device:TPU:0, one launch (start us, length us, event | category | flops | bytes accessed | tf_op | source)
XLA Modules:
  0.0 143.4 jit_solution(1472815727846049629)
XLA Ops:
  0.7 138.1 %layer.1 = (bf16[512,1024]{1,0:T(8,128)(2,1)}, f32[512,1024]{1,0:T(8,128)}, bf16[64,2048]{1,0:T(8,128)(2,1)}, bf16[256,512]{1,0:T(8,128)(2,1)}, bf16[64,512]{1,0...) custom-call(bf16[512,1024]{1,0:T(8,128)(2,1)} %bitcast.4, s32[1,512]{1,0:T(1,128)} %doc_hbm.1, ...), custom_call_target="tpu_custom_call" | custom-call | tf_op jit(solution)/shard_map/layer/pallas_call | solution.py:826
  138.8 4.4 %hand_over.1 = (bf16[512,1024]{1,0:T(8,128)(2,1)}, f32[512,1024]{1,0:T(8,128)}, f32[64,1536]{1,0:T(8,128)}, f32[1024]{0:T(1024)}, f32[1024]{0:T(1024)}, /*index=...) custom-call(bf16[512,1024]{1,0:T(8,128)(2,1)} %get-tuple-element.37., ...), custom_call_target="tpu_custom_call" | custom-call | tf_op jit(solution)/shard_map/hand_over/pallas_call | solution.py:878

commit v6 on v5

--- a/solution.py
+++ b/solution.py
@@ -685,7 +685,7 @@
         if i + 2 < 8:
             dload(i + 2).start()
 
-    for i in range(3):
+    for i in range(OUT_SPLIT[0]):
         out_part(i)
     for _ in range(N1_AFTER):
         serve()
@@ -733,12 +733,11 @@
         for _ in range(VEC_SERVES[i]):
             serve()
         if i == 0:
-            out_part(3)
-            out_part(4)
-            out_part(5)
+            for k in range(*OUT_SPLIT):
+                out_part(k)
         if i == 1:
-            out_part(6)
-            out_part(7)
+            for k in range(OUT_SPLIT[1], 8):
+                out_part(k)
             save_out.start()
         vec_copy(i).wait()
         total = vin[i, 0] + vin[i, 1]
@@ -783,7 +782,8 @@
 BACK_AT = 3
 SERVE_AT = (1, 3, 5)
 N1_AFTER = 1
-VEC_SERVES = (1, 1, 1, 1, 1)
+VEC_SERVES = (1, 2, 2, 2, 2)
+OUT_SPLIT = (3, 6)
 
 
 def vmem():

time: 144 us -> 141 us (0.979)
  Pallas kernels: 143 us -> 140 us
    pallas_call x1, Pallas kernels: 138 us -> 136 us  [fast_local(): pl.pallas_call(functools.partial(layer_kernel, halo), out_shape=(shape((t...]
where the time goes in v6:
time: 141 us
  Pallas kernels  140 us (99%)
    pallas_call x1, Pallas kernels, fast_local(): pl.pallas_call(functools.partial(layer_kernel, halo), out_shape=(shape((t...  136 us
    pallas_call x1, Pallas kernels, fast_local(): pl.pallas_call(finish_kernel, out_shape=return_shapes, in_specs=[vmem()]...  4.4 us

profile of v6, /device:TPU:0, one launch (start us, length us, event | category | flops | bytes accessed | tf_op | source)
XLA Modules:
  0.0 141.1 jit_solution(15115351851349882873)
XLA Ops:
  0.7 135.9 %layer.1 = (bf16[512,1024]{1,0:T(8,128)(2,1)}, f32[512,1024]{1,0:T(8,128)}, bf16[64,2048]{1,0:T(8,128)(2,1)}, bf16[256,512]{1,0:T(8,128)(2,1)}, bf16[64,512]{1,0...) custom-call(bf16[512,1024]{1,0:T(8,128)(2,1)} %bitcast.4, s32[1,512]{1,0:T(1,128)} %doc_hbm.1, ...), custom_call_target="tpu_custom_call" | custom-call | tf_op jit(solution)/shard_map/layer/pallas_call | solution.py:826
  136.5 4.4 %hand_over.1 = (bf16[512,1024]{1,0:T(8,128)(2,1)}, f32[512,1024]{1,0:T(8,128)}, f32[64,1536]{1,0:T(8,128)}, f32[1024]{0:T(1024)}, f32[1024]{0:T(1024)}, /*index=...) custom-call(bf16[512,1024]{1,0:T(8,128)(2,1)} %get-tuple-element.37., ...), custom_call_target="tpu_custom_call" | custom-call | tf_op jit(solution)/shard_map/hand_over/pallas_call | solution.py:878

commit v7 on v6

--- a/solution.py
+++ b/solution.py
@@ -827,11 +827,11 @@
         functools.partial(layer_kernel, halo),
         out_shape=(shape((tokens, width), BF16), shape((tokens, width), F32))
         + tuple(shape(dims, BF16) for dims in shards)
-        + (shape((16, width), F32),),
+        + (shape((12, width), F32),),
         in_specs=[hbm()] * 17,
         out_specs=(hbm(),) * 7,
         scratch_shapes=[pltpu.VMEM(dims, BF16) for dims in shards]
-        + [pltpu.VMEM((16, width), F32)]
+        + [pltpu.VMEM((12, width), F32)]
         + [pltpu.VMEM((tokens, width), BF16), pltpu.VMEM((1, tokens), jnp.int32), pltpu.VMEM((heads, 128), F32)]
         + [pltpu.VMEM((width,), BF16)] * 7
         + [pltpu.VMEM((ff,), BF16), pltpu.VMEM((width,), BF16)]
@@ -860,7 +860,7 @@
         ]
         + arrival_shapes(chunks)
         + [
-            pltpu.VMEM((5, 2, 16, width), F32),
+            pltpu.VMEM((5, 2, 12, width), F32),
             DMA((5,)), DMA((12,)), DMA((6,)), DMA((2,)), DMA((2, 4)), DMA, DMA((RING,)), DMA((chunks,)), DMA((4,)),
             DMA((4, chunks)), DMA((4,)), DMA((4,)), DMA((5,)), DMA((5,)), DMA((2,)),
         ],

time: 141 us -> 141 us (level)
  no operation moved by 1% of the time
where the time goes in v7:
time: 141 us
  Pallas kernels  140 us (99%)
    pallas_call x1, Pallas kernels, fast_local(): pl.pallas_call(functools.partial(layer_kernel, halo), out_shape=(shape((t...  136 us
    pallas_call x1, Pallas kernels, fast_local(): pl.pallas_call(finish_kernel, out_shape=return_shapes, in_specs=[vmem()]...  4.4 us

profile of v7, /device:TPU:0, one launch (start us, length us, event | category | flops | bytes accessed | tf_op | source)
XLA Modules:
  0.0 141.1 jit_solution(7448730743547154726)
XLA Ops:
  0.7 135.9 %layer.1 = (bf16[512,1024]{1,0:T(8,128)(2,1)}, f32[512,1024]{1,0:T(8,128)}, bf16[64,2048]{1,0:T(8,128)(2,1)}, bf16[256,512]{1,0:T(8,128)(2,1)}, bf16[64,512]{1,0...) custom-call(bf16[512,1024]{1,0:T(8,128)(2,1)} %bitcast.4, s32[1,512]{1,0:T(1,128)} %doc_hbm.1, ...), custom_call_target="tpu_custom_call" | custom-call | tf_op jit(solution)/shard_map/layer/pallas_call | solution.py:826
  136.5 4.4 %hand_over.1 = (bf16[512,1024]{1,0:T(8,128)(2,1)}, f32[512,1024]{1,0:T(8,128)}, f32[64,1536]{1,0:T(8,128)}, f32[1024]{0:T(1024)}, f32[1024]{0:T(1024)}, /*index=...) custom-call(bf16[512,1024]{1,0:T(8,128)(2,1)} %get-tuple-element.37., ...), custom_call_target="tpu_custom_call" | custom-call | tf_op jit(solution)/shard_map/hand_over/pallas_call | solution.py:878
